TPU v7x, 256 devices: a whole 4x4x8 slice. The times are simulated.
256 devices in a mesh: gx: 32 (over y, z), gy: 8 (over x, core).
Axes of the slice: x: 4, y: 4, z: 8, core: 2. Of those that a mesh axis runs over, the one named last changes fastest.
Arguments:
- right_side: float32 [512, 256, 128], P('gx', 'gy'), may hold values from -160 to 160
- beta: float32 [512, 256, 128], P('gx', 'gy'), may hold values from 1 to 10
- shift: float32 [512, 256, 128], P('gx', 'gy'), may hold values from 0.5 to 4
Outputs:
- corrected: float32 [512, 256, 128], P('gx', 'gy')
- middle: float32 [256, 128, 64], P('gx', 'gy')
All inputs are finite; a program needn't handle non-finite values.
Results may differ from a plain program's by a relative error of at most 0.00002.
Values sent between devices are 32-bit elements; how exact they have to be, the bound alone decides.
No kernel may reach another device: no remote copies, remote signals or barrier semaphores. Data moves between devices by JAX's collectives and lax.ppermute only.
A program may use at most 128 MiB of HBM per device.

v0:
```python
import jax
import jax.numpy as jnp
from jax import lax
from jax.experimental import pallas as pl
from jax.experimental.pallas import tpu as pltpu
from jax.sharding import PartitionSpec as P

SWEEPS = 4
THETA, DELTA = 1.15, 0.85
SIGMA = THETA / DELTA
F32 = jnp.float32


def coefficients():
    rho, out = 1.0 / SIGMA, []
    for _ in range(SWEEPS - 1):
        new = 1.0 / (2.0 * SIGMA - rho)
        out.append((new * rho, 2.0 * new / DELTA))
        rho = new
    return out


def lanes(rows):
    return lax.broadcasted_iota(jnp.int32, (rows, 128), 1)


def roll(value, shift):
    return pltpu.roll(value, shift % 128, 1)


class StepSplit:
    def __init__(self, inner, outer, planes, level):
        self.inner, self.outer, self.planes, self.level, self.own = inner, outer, planes, level, set()

    def __getitem__(self, at):
        return (self.inner if at[0] in self.planes and at[0] not in self.own else self.outer)[at]

    def __setitem__(self, at, value):
        self.outer[at] = value
        if at[1].start >= self.level.bases[-1]:
            self.own.add(at[0])


class Level:
    def __init__(self, depth, own_planes, rows, own_rows, rep, folded=False, bases=(0,)):
        self.bases = bases
        self.depth, self.own, self.rep, self.folded = depth, own_planes, rep, folded
        self.planes = depth + own_planes // 2 if folded else own_planes + 2 * depth
        self.rows, self.first_row, self.own_rows = rows, (rows - own_rows) // 2, own_rows

    def cut(self, k):
        return k, self.planes - (0 if self.folded else k)

    def span(self, plane, reach):
        x = plane - self.depth
        far = max(0, -x) if self.folded else max(0, -x, x - self.own + 1)
        side = max(0, reach - far)
        lo = max(0, self.first_row - side) // 8 * 8
        hi = min(self.rows, -(-(self.first_row + self.own_rows + side) // 8) * 8)
        return lo, hi - lo

    def put(self, dst, i, at, value):
        dst[i, at, :] = value
        if self.folded and i == self.planes - 1:
            dst[i + 1, at, :] = swap_lanes(value)


def swap_lanes(value):
    return jnp.where(lanes(value.shape[0]) % 2 == 0, roll(value, -1), roll(value, 1))


def build(level, scale, beta, rhs, shift, work, planes=None):
    wx, wy, wym, wz, wzm, diag, inv, rhs_n, start = work
    rep, half, last_span = level.rep, 0.5 * scale, None
    planes = range(level.planes) if planes is None else planes
    for base, i in [(base, i) for base in level.bases for i in planes]:
        lo, n = level.span(i, level.depth)
        lo += base
        if (lo, n, i) != last_span:
            prev, cur = beta[i, pl.ds(8 + lo, n), :], beta[i + 1, pl.ds(8 + lo, n), :]
            wx_prev = half * (prev + cur)
            if i:
                wx[i - 1, pl.ds(lo, n), :] = wx_prev
            lane = lanes(n)
            first, last = lane < rep, lane >= 128 - rep
        last_span = (lo, n, i + 1)
        at = pl.ds(lo, n)
        nxt = beta[i + 2, pl.ds(8 + lo, n), :]
        wx_next = half * (cur + nxt)
        w_up = half * (cur + beta[i + 1, pl.ds(9 + lo, n), :])
        w_down = half * (cur + beta[i + 1, pl.ds(7 + lo, n), :])
        w_right = half * (cur + jnp.where(last, 0.0, roll(cur, -rep)))
        w_left = half * (cur + jnp.where(first, 0.0, roll(cur, rep)))
        d = shift(i, at) + (wx_prev + wx_next + w_up + w_down + w_right + w_left)
        iv = jnp.where(cur > 0.0, 1.0 / d, 0.0)
        wx[i, at, :] = wx_next
        wy[i, at, :] = w_up
        wym[i, at, :] = w_down
        wz[i, at, :] = jnp.where(last, 0.0, w_right)
        wzm[i, at, :] = jnp.where(first, 0.0, w_left)
        diag[i, at, :] = d
        inv[i, at, :] = iv
        if rhs is not None:
            begin(level, i, lo, n, rhs, iv, rhs_n, start)
        cur, wx_prev = nxt, wx_next


def begin(level, i, lo, n, rhs, iv, rhs_n, start):
    c = rhs(i, pl.ds(lo, n)) * iv
    rhs_n[i, pl.ds(lo, n), :] = c
    level.put(start, i, pl.ds(8 + lo, n), c * (1.0 / THETA))


def scaled_residual(level, src, planes, reach, work, emit):
    wx, wy, wym, wz, wzm, _, inv, rhs_n, _ = work
    rep, last_span = level.rep, None
    for base, i in [(base, i) for base in level.bases for i in planes]:
        lo, n = level.span(i, reach)
        lo += base
        at, dom = pl.ds(lo, n), pl.ds(8 + lo, n)
        if (lo, n, i) != last_span:
            prev, cur, wx_prev = src[i - 1, dom, :], src[i, dom, :], wx[i - 1, at, :]
        last_span = (lo, n, i + 1)
        nxt, wx_next = src[i + 1, dom, :], wx[i, at, :]
        t = wx_next * nxt + wx_prev * prev
        t = t + wy[i, at, :] * src[i, pl.ds(9 + lo, n), :] + wym[i, at, :] * src[i, pl.ds(7 + lo, n), :]
        t = t + wz[i, at, :] * roll(cur, -rep) + wzm[i, at, :] * roll(cur, rep)
        emit(i, lo, n, cur, rhs_n[i, at, :] + inv[i, at, :] * t - cur)
        prev, cur, wx_prev = cur, nxt, wx_next


def sweeps(level, work, fields, step, planes):
    for k, (a, g) in enumerate(coefficients()):

        def emit(i, lo, n, cur, e, a=a, g=g, k=k, dst=fields[k + 1]):
            before = cur if k == 0 else step[i, pl.ds(lo, n), :]
            d = a * before + g * e
            if k < SWEEPS - 2:
                step[i, pl.ds(lo, n), :] = d
            level.put(dst, i, pl.ds(8 + lo, n), cur + d)

        scaled_residual(level, fields[k], planes(k + 1), level.depth - k - 1, work, emit)
    return fields[-1]


def smooth(level, work, other, step):
    fields = (work[8], other) * 2
    return sweeps(level, work, fields, step, lambda k: range(*level.cut(k)))


class Split:
    def __init__(self, inner, outer, first, last):
        self.inner, self.outer, self.first, self.last = inner, outer, first, last

    def __getitem__(self, at):
        return (self.inner if self.first <= at[0] <= self.last else self.outer)[at]

    def __setitem__(self, at, value):
        if not self.first <= at[0] <= self.last:
            self.outer[at] = value


FINE = Level(4, 16, 32, 32, 1)
STRIP = Level(4, 16, 16, 16, 1, bases=(0, 24))
MID = Level(10, 8, 40, 16, 2, folded=True)
LOW = Level(3, 4, 16, 8, 4, folded=True)


def table(entries):
    rows, at = {}, 0
    for key, count in entries:
        rows[key] = (at, count)
        at += count
    return rows, -(-at // 8) * 8


FACE_Y, FACE_Y_SIZE = table([((f, x), 8) for x in range(16) for f in (0, 2)] + [((1, x), 9) for x in range(16)])

MID_Y = {0: 4, 1: 4, 2: 3}
HALO_X = [-1, -2, -3, -4, -5, 16, 17, 18, 19, 20]


def away(x):
    return -x if x < 0 else x - 15


SECOND_Y, SECOND_Y_SIZE = table(
    [((f, "mid", m), MID_Y[f]) for f in range(3) for m in range(8)]
    + [((f, "fine", x), 8 + (f == 1) - away(x)) for f in range(3) for x in HALO_X if away(x) < 5 + (f == 1)]
)


def side_rows(field, far):
    return -(-max(0, 10 + (field == 1) - far) // 2)


NEAR_X, NEAR_X_SIZE = table([((f, d), 8 + 2 * side_rows(f, d)) for f in range(3) for d in range(1, 9)])
FAR_X, FAR_X_SIZE = table([((f, d), 8 + 2 * side_rows(f, d)) for f in range(3) for d in range(9, 11 + (f == 1))])


def flag(condition):
    return jnp.where(condition, 1.0, 0.0).astype(F32)


def x_flags():
    i, n = lax.axis_index("gx"), lax.axis_size("gx")
    return {-2: flag(i > 1), -1: flag(i > 0), 1: flag(i < n - 1), 2: flag(i < n - 2)}


def y_flags():
    j, n = lax.axis_index("gy"), lax.axis_size("gy")
    return flag(j > 0), flag(j < n - 1)


def upward(axis, by, low=0):
    return lax.rem(lax.axis_index(axis) + low * by, 2 * by) >= by


def swaps(first, second, axis, by, low=0):
    axes = ("gx", "gy")
    size = [lax.axis_size(name) for name in axes]
    dim = axes.index(axis)
    orders = []
    for sign in (1, -1):
        pairs = []
        for i in range(size[0]):
            for j in range(size[1]):
                to = [i, j]
                to[dim] += sign * by if (to[dim] + low * by) % (2 * by) >= by else -sign * by
                if not 0 <= to[dim] < size[dim]:
                    to = [i, j]
                    to[1 - dim] ^= 1
                pairs.append((i * size[1] + j, to[0] * size[1] + to[1]))
        orders.append(pairs)
    return lax.ppermute(first, axes, orders[0]), lax.ppermute(second, axes, orders[1])


COUNTS = (4, 5, 4)
STARTS = (0, 4, 9)


def pack_fine_x(fields):
    ends = [f[:n] for f, n in zip(fields, COUNTS)] + [f[16 - n:] for f, n in zip(fields, COUNTS)]
    first, last = jnp.concatenate(ends[:3], axis=0), jnp.concatenate(ends[3:], axis=0)
    first, last = lax.optimization_barrier((first, last))
    up = upward("gx", 1)
    return jnp.where(up, last, first), jnp.where(up, first, last)


def fine_plane(field, x, own, in_a, in_b, up):
    if 0 <= x < 16:
        return own[field][x]
    i = STARTS[field] + (x + COUNTS[field] if x < 0 else x - 16)
    return jnp.where(up, in_b[i], in_a[i]) if x < 0 else jnp.where(up, in_a[i], in_b[i])


def pick(ref, rows, key):
    at, count = rows[key]
    return ref[pl.ds(at, count), :]


def put_both(out_a, out_b, rows, key, up, higher, lower):
    at, count = rows[key]
    out_a[pl.ds(at, count), :] = jnp.where(up, higher, lower)
    out_b[pl.ds(at, count), :] = jnp.where(up, lower, higher)


def pack_face_y(b, beta, shift, out_a, out_b, packed, pair):
    up = upward("gy", 1)
    for field, src in ((1, beta), (2, shift)):
        for m in range(8):
            at = 8 * field + m - 8
            pair[at] = src[2 * m] + src[2 * m + 1]
            packed[field - 1, m] = pack_pairs(pair, at, 0, 8)
    for field, src in enumerate((b, beta, shift)):
        for x in range(16):
            n = FACE_Y[field, x][1]
            put_both(out_a, out_b, FACE_Y, (field, x), up, src[x, pl.ds(32 - n, n), :], src[x, pl.ds(0, n), :])


def y_sides(rows, key, in_a, in_b, up):
    a, b = pick(in_a, rows, key), pick(in_b, rows, key)
    return jnp.where(up, b, a), jnp.where(up, a, b)


def pack_pairs(pair, plane, start, count):
    even = lanes(count) % 2 == 0
    e = pair[plane, pl.ds(start, count, 4), :] + pair[plane, pl.ds(start + 1, count, 4), :]
    o = pair[plane, pl.ds(start + 2, count, 4), :] + pair[plane, pl.ds(start + 3, count, 4), :]
    return jnp.where(even, e + roll(e, -1), o + roll(o, 1)) * 0.125


def pair_residual(level, src, work, pair, first, planes):
    diag, held = work[5], {}

    def emit(i, lo, n, cur, e):
        r = e * diag[i, pl.ds(lo, n), :]
        if i % 2 == 0:
            held[0] = r
        else:
            pair[first + (i - 4) // 2, pl.ds(lo, n), :] = held[0] + r

    scaled_residual(level, src, planes, 0, work, emit)


def INNER(k):
    return range(5 + k, 19 - k)


def rest(k):
    return [i for i in range(k, 24 - k) if i not in INNER(k)]


def split_work(inner, outer, level):
    work = tuple(Split(i, o, 5, 18) for i, o in zip(inner[:9], outer[:9]))
    fields = [work[8]]
    for k in (1, 2, 3):
        fields.append(Split(inner[8 + k], outer[8 + k], INNER(k)[0], INNER(k)[-1]))
    step = StepSplit(inner[12], outer[12], INNER(1), level)
    return work, fields, step, Split(inner[13], outer[13], 3, 4)


def edge_rows(be, x, beta, ya_in, yb_in):
    (low, high), up = y_flags(), upward("gy", 1)
    lo, hi = y_sides(FACE_Y, (1, x), ya_in, yb_in, up)
    be[x + 5, 8:40, :] = beta[x]
    be[x + 5, 7:8, :] = lo[8:9] * low
    be[x + 5, 40:41, :] = hi[0:1] * high


def inner_kernel(
    b, beta, shift, ya_in, yb_in,
    wx, wy, wym, wz, wzm, diag, inv, rhs_n, x0, x1, x2, x3, step, pair, be,
):
    for x in range(16):
        edge_rows(be, x, beta, ya_in, yb_in)
    work = (wx, wy, wym, wz, wzm, diag, inv, rhs_n, x0)
    build(FINE, 1.0, be, lambda i, at: b[i - 4], lambda i, at: shift[i - 4], work, INNER(0))
    sweeps(FINE, work, (x0, x1, x2, x3), step, INNER)
    pair_residual(FINE, x3, work, pair, 0, range(10, 14))


def outer_kernel(
    b, beta, shift, coarse, xa_in, xb_in, ya_in, yb_in, *refs,
):
    inner, refs = refs[:14], refs[14:]
    (x_out, packed, out_a, out_b, be, bb, ss), outer = refs[:7], refs[7:]
    near, up_x, up_y = x_flags(), upward("gx", 1), upward("gy", 1)
    own = (b, beta, shift)
    for x in [*range(-5, 2), *range(14, 21)]:
        if 0 <= x < 16:
            edge_rows(be, x, beta, ya_in, yb_in)
            continue
        p = fine_plane(1, x, own, xa_in, xb_in, up_x)
        be[x + 5, 8:40, :] = p * (near[-1] if x < 0 else near[1])
        at = SECOND_Y[1, "fine", x][1]
        put_both(out_a, out_b, SECOND_Y, (1, "fine", x), up_y, p[32 - at:32], p[0:at])
    for field, dst in ((0, bb), (2, ss)):
        for x in [*range(-4, 0), *range(16, 20)]:
            p = fine_plane(field, x, own, xa_in, xb_in, up_x)
            dst[x + 4] = p
            at = SECOND_Y[field, "fine", x][1]
            put_both(out_a, out_b, SECOND_Y, (field, "fine", x), up_y, p[32 - at:32], p[0:at])
    work, fields, step, pair = split_work(inner, outer, FINE)

    def plane_of(src, halo):
        return lambda i, at: src[i - 4] if 4 <= i < 20 else halo[i]

    build(FINE, 1.0, be, plane_of(b, bb), plane_of(shift, ss), work, rest(0))
    x = sweeps(FINE, work, fields, step, rest)
    pair_residual(FINE, x, work, pair, 0, [*range(4, 10), *range(14, 20)])
    for m in range(8):
        packed[m] = pack_pairs(pair, m, 0, 8)
        put_both(out_a, out_b, SECOND_Y, (0, "mid", m), up_y, packed[m, 3:7, :], packed[m, 1:5, :])
        for field in (1, 2):
            n = MID_Y[field]
            higher, lower = coarse[field - 1, m, 6 - n:6, :], coarse[field - 1, m, 2:2 + n, :]
            put_both(out_a, out_b, SECOND_Y, (field, "mid", m), up_y, higher, lower)
    for i in range(16):
        x_out[i] = x[i + 4, pl.ds(8, 32), :]


def strip_kernel(
    b, beta, shift, packed, ya_in, yb_in,
    wx, wy, wym, wz, wzm, diag, inv, rhs_n, x0, x1, x2, x3, step, pair, ext, be, bb, ss, sums,
):
    (low, high), up_y = y_flags(), upward("gy", 1)
    for x in range(16):
        lo, hi = y_sides(FACE_Y, (1, x), ya_in, yb_in, up_y)
        be[x + 5, 16:25, :] = beta[x, 0:9, :]
        be[x + 5, 31:40, :] = beta[x, 23:32, :]
        be[x + 5, 7:16, :] = lo * low
        be[x + 5, 40:49, :] = hi * high
    for field, src, dst in ((0, b, bb), (2, shift, ss)):
        for x in range(16):
            lo, hi = y_sides(FACE_Y, (field, x), ya_in, yb_in, up_y)
            dst[x + 4, 8:16, :] = src[x, 0:8, :]
            dst[x + 4, 24:32, :] = src[x, 24:32, :]
            dst[x + 4, 0:8, :] = lo
            dst[x + 4, 32:40, :] = hi
    work = (wx, wy, wym, wz, wzm, diag, inv, rhs_n, x0)
    build(STRIP, 1.0, be, lambda i, at: bb[i, at, :], lambda i, at: ss[i, at, :], work, INNER(0))
    sweeps(STRIP, work, (x0, x1, x2, x3), step, INNER)
    pair_residual(STRIP, x3, work, pair, 0, range(10, 14))

    for m in range(8):
        sums[m] = be[2 * m + 5] + be[2 * m + 6]
        sums[m + 8, 0:40, :] = ss[2 * m + 4] + ss[2 * m + 5]
        for field, plane, at in ((1, m, 8), (2, m + 8, 0)):
            dst = ext.at[field - 1, m]
            dst[4:6, :] = pack_pairs(sums, plane, at, 2)
            dst[6:14, :] = packed[field - 1, m]
            dst[14:16, :] = pack_pairs(sums, plane, at + 32, 2)


def edge_kernel(
    b, beta, shift, xa_in, xb_in, ya_in, yb_in, packed, ya2, yb2, *refs,
):
    inner, ext_c, refs = refs[:14], refs[14], refs[15:]
    (x_out, ext, near_a, near_b, far_a, far_b, be, bb, ss), outer = refs[:9], refs[9:]
    near, (low, high) = x_flags(), y_flags()
    up_x, up_y = upward("gx", 1), upward("gy", 1)
    own = (b, beta, shift)

    def sides(field, x):
        if 0 <= x < 16:
            return y_sides(FACE_Y, (field, x), ya_in, yb_in, up_y)
        return y_sides(SECOND_Y, (field, "fine", x), ya2, yb2, up_y)

    for x in [*range(-5, 2), *range(14, 21)]:
        p = fine_plane(1, x, own, xa_in, xb_in, up_x)
        lo, hi = sides(1, x)
        n = lo.shape[0]
        f = 1.0 if 0 <= x < 16 else near[-1] if x < 0 else near[1]
        if not 0 <= x < 16:
            p = p * f
        be[x + 5, 16:25, :] = p[0:9]
        be[x + 5, 31:40, :] = p[23:32]
        be[x + 5, pl.ds(16 - n, n), :] = lo * (low * f)
        be[x + 5, pl.ds(40, n), :] = hi * (high * f)
    for field, dst in ((0, bb), (2, ss)):
        for x in [*range(-4, 1), *range(15, 20)]:
            p = fine_plane(field, x, own, xa_in, xb_in, up_x)
            lo, hi = sides(field, x)
            n = lo.shape[0]
            dst[x + 4, 8:16, :] = p[0:8]
            dst[x + 4, 24:32, :] = p[24:32]
            dst[x + 4, pl.ds(8 - n, n), :] = lo
            dst[x + 4, pl.ds(32, n), :] = hi
    work, fields, step, pair = split_work(inner, outer, STRIP)
    build(STRIP, 1.0, be, lambda i, at: bb[i, at, :], lambda i, at: ss[i, at, :], work, rest(0))
    x = sweeps(STRIP, work, fields, step, rest)
    pair_residual(STRIP, x, work, pair, 0, [*range(4, 10), *range(14, 20)])
    for m in range(8):
        lo, hi = y_sides(SECOND_Y, (0, "mid", m), ya2, yb2, up_y)
        ext[0, m, 1:5, :] = lo
        ext[0, m, 5:7, :] = pack_pairs(pair, m, 4, 2)
        ext[0, m, 7:13, :] = packed[m, 1:7, :]
        ext[0, m, 13:15, :] = pack_pairs(pair, m, 28, 2)
        ext[0, m, 15:19, :] = hi
        for field in (1, 2):
            n = MID_Y[field]
            lo, hi = y_sides(SECOND_Y, (field, "mid", m), ya2, yb2, up_y)
            ext[field, m, 4 - n:4, :] = lo * low if field == 1 else lo
            ext[field, m, 4:16, :] = ext_c[field - 1, m, 4:16, :]
            ext[field, m, 16:16 + n, :] = hi * high if field == 1 else hi
    up2 = upward("gx", 2)
    for rows, up, a, c, first in ((NEAR_X, upward("gx", 1, 1), near_a, near_b, 1), (FAR_X, up2, far_a, far_b, 9)):
        for field, d in rows:
            n = side_rows(field, d)
            at = pl.ds(6 - n, 8 + 2 * n)
            higher, lower = ext[field, 8 - d + (first - 1), at, :], ext[field, d - first, at, :]
            put_both(a, c, rows, (field, d), up, higher, lower)
    for i in range(16):
        x_out[i, 0:4, :] = x[i + 4, pl.ds(16, 4), :]
        x_out[i, 4:8, :] = x[i + 4, pl.ds(36, 4), :]


def spread(dst, plane, start, a, b):
    n = a.shape[0]
    even = lanes(n) % 2 == 0
    dst[plane, pl.ds(start, n, 2), :] = jnp.where(even, a, roll(b, 1))
    dst[plane, pl.ds(start + 1, n, 2), :] = jnp.where(even, roll(a, -1), b)


def gather(field, d, ext, near, far=None):
    if d <= 0:
        n = side_rows(field, 0)
        at = pl.ds(6 - n, 8 + 2 * n)
        return ext[field, -d, at, :], ext[field, 7 + d, at, :]
    hop, rows, (a, c) = (1, NEAR_X, near) if d <= 8 else (2, FAR_X, far)
    u = upward("gx", hop, 2 - hop)
    a, c = pick(a, rows, (field, d)), pick(c, rows, (field, d))
    lower, higher = jnp.where(u, c, a), jnp.where(u, a, c)
    if field == 1:
        flags = x_flags()
        return lower * flags[-hop], higher * flags[hop]
    return lower, higher


def unpack_mid(field, planes, dst, first, reach, *messages):
    for i in planes:
        a, b = gather(field, reach - i, *messages)
        spread(dst, i, first - (a.shape[0] - 8), a, b)


def down_sample(pair, plane):
    low_pair = lanes(16) % 4 < 2
    s = pair[plane, pl.ds(4, 16, 2), :] + pair[plane, pl.ds(5, 16, 2), :]
    return (s + jnp.where(low_pair, roll(s, -2), roll(s, 2))) * 0.125


def pair_mid_residual(src, work, pair, planes):
    diag, held = work[5], {}

    def emit(i, lo, n, cur, e):
        r = e * diag[i, pl.ds(lo, n), :]
        if i % 2 == 0:
            held[0] = lo, n, r
        else:
            lo0, n0, r0 = held[0]
            at, end = max(lo, lo0), min(lo + n, lo0 + n0)
            total = r0[at - lo0:end - lo0] + r[at - lo:end - lo]
            pair[(i - 4) // 2, pl.ds(at, end - at), :] = total

    scaled_residual(MID, src, planes, 6, work, emit)


def MID_INNER(k):
    return range(3 + k, 14)


def mid_kernel(
    ext, near_a, near_b,
    wx, wy, wym, wz, wzm, diag, inv, rhs_n, x0, x1, x2, x3, step, pair,
    wx2, wy2, wym2, wz2, wzm2, diag2, inv2,
    be, bb, ss, be2, ss2, sums,
):
    messages = ext, (near_a, near_b)
    unpack_mid(1, range(3, 15), be, 20, 11, *messages)
    unpack_mid(0, range(3, 14), bb, 12, 10, *messages)
    unpack_mid(2, range(3, 14), ss, 12, 10, *messages)
    be[15, pl.ds(8, 40), :] = swap_lanes(be[14, pl.ds(8, 40), :])
    work = (wx, wy, wym, wz, wzm, diag, inv, rhs_n, x0)
    build(MID, 0.25, be, lambda i, at: bb[i, at, :], lambda i, at: ss[i, at, :], work, MID_INNER(0))
    sweeps(MID, work, (x0, x1, x2, x3), step, MID_INNER)
    pair_mid_residual(x3, work, pair, range(8, 14))

    for m in range(6):
        sums[m] = be[2 * m + 3, pl.ds(8, 40), :] + be[2 * m + 4, pl.ds(8, 40), :]
    for m in range(5):
        sums[6 + m] = ss[2 * m + 4] + ss[2 * m + 5]
    for m in range(6):
        be2[m, 8:24, :] = down_sample(sums, m)
    be2[6, 8:24, :] = swap_lanes(be2[5, 8:24, :])
    for m in range(5):
        ss2[m] = down_sample(sums, 6 + m)
    work2 = (wx2, wy2, wym2, wz2, wzm2, diag2, inv2, None, None)
    build(LOW, 0.0625, be2, None, lambda i, at: ss2[i, at, :], work2)


def coarse_kernel(
    x_fine, x_edge, ext, near_a, near_b, far_a, far_b,
    i_wx, i_wy, i_wym, i_wz, i_wzm, i_diag, i_inv, i_rhs_n, i_x0, i_x1, i_x2, i_x3, i_step, i_pair,
    wx2, wy2, wym2, wz2, wzm2, diag2, inv2,
    out, mid_out,
    be, bb, ss, wx, wy, wym, wz, wzm, diag, inv, rhs_n, x0, x1, x2, x3, step, pair,
    rhs_n2, xa2, xb2, step2, rep_mid, rep_fine, mids,
):
    messages = ext, (near_a, near_b), (far_a, far_b)
    unpack_mid(1, range(5), be, 20, 11, *messages)
    unpack_mid(0, range(3), bb, 12, 10, *messages)
    unpack_mid(2, range(3), ss, 12, 10, *messages)
    inner = (i_wx, i_wy, i_wym, i_wz, i_wzm, i_diag, i_inv, i_rhs_n, i_x0)
    outer = (wx, wy, wym, wz, wzm, diag, inv, rhs_n, x0)
    work = tuple(Split(i, o, 3, 14) for i, o in zip(inner, outer))
    fields = [work[8]] + [Split(i, o, 3 + k, 14) for k, i, o in ((1, i_x1, x1), (2, i_x2, x2), (3, i_x3, x3))]

    def rest(k):
        return range(k, 3 + k)

    build(MID, 0.25, be, lambda i, at: bb[i, at, :], lambda i, at: ss[i, at, :], work, rest(0))
    x1 = sweeps(MID, work, fields, StepSplit(i_step, step, MID_INNER(1), MID), rest)
    pair = Split(i_pair, pair, 2, 4)
    pair_mid_residual(x1, work, pair, range(4, 8))
    for i in range(LOW.planes):
        lo, n = LOW.span(i, LOW.depth)
        begin(LOW, i, lo, n, lambda i, at: down_sample(pair, i), inv2[i], rhs_n2, xa2)
    work2 = (wx2, wy2, wym2, wz2, wzm2, diag2, inv2, rhs_n2, xa2)
    x2 = smooth(LOW, work2, xb2, step2)

    for m in range(2):
        low_x = x2[m + 3, pl.ds(12, 8), :]
        rep_mid[m, pl.ds(0, 8, 2), :] = low_x
        rep_mid[m, pl.ds(1, 8, 2), :] = low_x
    even = lanes(16) % 2 == 0
    for m in range(4):
        both = x1[m + 10, pl.ds(20, 16), :] + rep_mid[m // 2]
        for x, mid in (
            (m, jnp.where(even, both, roll(both, 1))),
            (7 - m, jnp.where(even, roll(both, -1), both)),
        ):
            mids[pl.ds(16 * x, 16), :] = mid
            rep_fine[x, pl.ds(0, 16, 2), :] = mid
            rep_fine[x, pl.ds(1, 16, 2), :] = mid
    for i in range(16):
        out[i, 4:28, :] = x_fine[i, 4:28, :] + rep_fine[i // 2, 4:28, :]
        out[i, 0:4, :] = x_edge[i, 0:4, :] + rep_fine[i // 2, 0:4, :]
        out[i, 28:32, :] = x_edge[i, 4:8, :] + rep_fine[i // 2, 28:32, :]
    row = lax.broadcasted_iota(jnp.int32, (128, 64), 0)
    col = lax.broadcasted_iota(jnp.int32, (128, 64), 1)
    even_lanes = jnp.where(row == 2 * col, 1.0, 0.0).astype(F32)
    compact = jnp.dot(mids[...], even_lanes, precision=lax.Precision.HIGHEST, preferred_element_type=F32)
    for m in range(8):
        mid_out[m] = compact[16 * m:16 * m + 16]


def vmem(*shape):
    return pltpu.VMEM(shape, F32)


def call(kernel, ins, outs, scratch=(), limit=24 * 2**20, space=pltpu.VMEM):
    return pl.pallas_call(
        kernel,
        out_shape=[jax.ShapeDtypeStruct(s, F32) for s in outs],
        in_specs=[pl.BlockSpec(memory_space=space)] * len(ins),
        out_specs=[pl.BlockSpec(memory_space=pltpu.VMEM)] * len(outs),
        scratch_shapes=list(scratch),
        compiler_params=pltpu.CompilerParams(vmem_limit_bytes=limit),
    )(*ins)


def work_shapes(planes, rows, pairs):
    flat, tall = (planes, rows, 128), (planes + 1, rows + 16, 128)
    return [flat] * 8 + [tall] * 4 + [flat, (pairs, rows, 128)]


def level_scratch(planes, rows):
    return [vmem(planes + 2, rows + 16, 128)] + [vmem(planes, rows, 128)] * 2


def work_scratch(planes, rows, pairs):
    return [vmem(*shape) for shape in work_shapes(planes, rows, pairs)]


def local(b, beta, shift):
    fields = (b, beta, shift)
    a, c = pack_fine_x(fields)
    xs = swaps(a, c, "gx", 1)
    a, c, packed_c = call(
        pack_face_y, fields, [(FACE_Y_SIZE, 128)] * 2 + [(2, 8, 8, 128)], [vmem(16, 32, 128)]
    )
    ys = swaps(a, c, "gy", 1)
    inner = call(inner_kernel, (*fields, *ys), work_shapes(24, 32, 8), [vmem(26, 48, 128)])
    x_fine, packed, a, c = call(
        outer_kernel,
        (*fields, packed_c, *xs, *ys, *inner),
        [(16, 32, 128), (8, 8, 128)] + [(SECOND_Y_SIZE, 128)] * 2,
        level_scratch(24, 32) + work_scratch(24, 32, 8),
    )
    second = swaps(a, c, "gy", 1)
    *inner, ext_c = call(
        strip_kernel,
        (*fields, packed_c, *ys),
        work_shapes(24, 40, 8) + [(2, 8, 24, 128)],
        level_scratch(24, 40) + [vmem(16, 56, 128)],
    )
    x_edge, ext, near_a, near_b, far_a, far_b = call(
        edge_kernel,
        (*fields, *xs, *ys, packed, *second, *inner, ext_c),
        [(16, 8, 128), (3, 8, 24, 128)] + [(NEAR_X_SIZE, 128)] * 2 + [(FAR_X_SIZE, 128)] * 2,
        level_scratch(24, 40) + work_scratch(24, 40, 8),
    )
    near = swaps(near_a, near_b, "gx", 1, 1)
    far = swaps(far_a, far_b, "gx", 2)
    small = (5, 16, 128)
    inner = call(
        mid_kernel,
        (ext, *near),
        work_shapes(14, 40, 5) + [small] * 7,
        level_scratch(14, 40) + [vmem(7, 32, 128), vmem(*small), vmem(11, 40, 128)],
    )
    return tuple(call(
        coarse_kernel,
        (x_fine, x_edge, ext, *near, *far, *inner),
        [(16, 32, 128), (8, 16, 64)],
        level_scratch(14, 40) + work_scratch(14, 40, 5)
        + [vmem(*small), vmem(6, 32, 128), vmem(6, 32, 128), vmem(*small)]
        + [vmem(2, 16, 128), vmem(8, 32, 128), vmem(128, 128)],
    ))


def solution(mesh):
    placed = P("gx", "gy", None)
    return jax.shard_map(
        local, mesh=mesh, in_specs=(placed,) * 3, out_specs=(placed, placed), check_vma=False
    )
```

profile of v0, /device:TPU:24, one launch (start us, length us, event | category | flops | bytes accessed | tf_op | source)
XLA Modules:
  0.0 34.2 jit_solution(22234893449575253)
XLA Ops:
  0.7 0.9 %fusion = (f32[4,32,128]{2,1,0:T(8,128)S(1)}, f32[4,32,128]{2,1,0:T(8,128)S(1)}) fusion(f32[16,32,128]{2,1,0:T(8,128)} %b.9), kind=kLoop, calls=%fused_computation.4 | loop fusion | bytes 262144 | tf_op jit(solution)/shard_map/slice | solution.py:243
  1.6 0.1 copy-done
  1.8 2.0 %collective-permute-start.1 = (f32[13,32,128]{2,1,0:T(8,128)S(1)}, f32[13,32,128]{2,1,0:T(8,128)S(1)}, u32[]{:S(2)}, u32[]{:S(2)}) collective-permute-start(f32[13,32,128]{2,1,0:T(8,128)S(1)} %get-tuple-element.132), channel_id=1, source_target_pairs={{0,8},{1,9},{2,10},{3,11},{4,12},{5,13},{6,14},{7,15},{8,0},{9,1},... | collective-permute-start | bytes 638984 | tf_op jit(solution)/shard_map/ppermute | solution.py:235
  3.8 5.1 %collective-permute-start = (f32[13,32,128]{2,1,0:T(8,128)S(1)}, f32[13,32,128]{2,1,0:T(8,128)S(1)}, u32[]{:S(2)}, u32[]{:S(2)}) collective-permute-start(f32[13,32,128]{2,1,0:T(8,128)S(1)} %get-tuple-element.133), channel_id=1, source_target_pairs={{0,1},{1,0},{2,3},{3,2},{4,5},{5,4},{6,7},{7,6},{8,16},{9,17},{10,... | collective-permute-start | bytes 638984 | tf_op jit(solution)/shard_map/ppermute | solution.py:235
  9.0 0.1 shard_map.50
  9.1 0.1 collective-permute-start.2
  9.2 1.6 %collective-permute-start.3 = (f32[400,128]{1,0:T(8,128)S(1)}, f32[400,128]{1,0:T(8,128)S(1)}, u32[]{:S(2)}, u32[]{:S(2)}) collective-permute-start(f32[400,128]{1,0:T(8,128)S(1)} %get-tuple-element.71), channel_id=1, source_target_pairs={{0,1},{1,0},{2,3},{3,2},{4,5},{5,4},{6,7},{7,6},{8,9},{9,8},{10,11... | collective-permute-start | bytes 614408 | tf_op jit(solution)/shard_map/ppermute | solution.py:235
  10.8 4.2 %collective-permute-done.2.ya_in = f32[400,128]{1,0:T(8,128)S(1)} collective-permute-done((f32[400,128]{1,0:T(8,128)S(1)}, f32[400,128]{1,0:T(8,128)S(1)}, u32[]{:S(2)}, u32[]{:S(2)}) %collective-permute-start.2) | collective-permute-done | bytes 204832 | tf_op jit(solution)/shard_map/ppermute | solution.py:235
  14.9 0.7 %shard_map.51 = (f32[24,32,128]{2,1,0:T(8,128)S(1)}, f32[24,32,128]{2,1,0:T(8,128)S(1)}, f32[24,32,128]{2,1,0:T(8,128)S(1)}, f32[24,32,128]{2,1,0:T(8,128)S(1)},...) custom-call(f32[16,32,128]{2,1,0:T(8,128)S(1)} %copy-done.1, ...), custom_call_target="tpu_custom_call" | custom-call | tf_op jit(solution)/shard_map/pallas_call | solution.py:623
  15.7 0.9 %shard_map.52 = (f32[16,32,128]{2,1,0:T(8,128)S(1)}, f32[8,8,128]{2,1,0:T(8,128)S(1)}, f32[240,128]{1,0:T(8,128)S(1)}, f32[240,128]{1,0:T(8,128)S(1)}) custom-call(f32[16,32,128]{2,1,0:T(8,128)S(1)} %copy-done.1, f32[16,32,128]{2,1,0:T(8,128)S(1)} %copy-done, f32[16,32,128]{2,1,0:T(8,128)S(1)} %copy-done.2, ...), custom_call_target="tpu_custom_call" | custom-call | tf_op jit(solution)/shard_map/pallas_call | solution.py:623
  16.6 0.1 collective-permute-start.4
  16.7 1.0 %collective-permute-start.5 = (f32[240,128]{1,0:T(8,128)S(1)}, f32[240,128]{1,0:T(8,128)S(1)}, u32[]{:S(2)}, u32[]{:S(2)}) collective-permute-start(f32[240,128]{1,0:T(8,128)S(1)} %get-tuple-element.89), channel_id=1, source_target_pairs={{0,1},{1,0},{2,3},{3,2},{4,5},{5,4},{6,7},{7,6},{8,9},{9,8},{10,11... | collective-permute-start | bytes 368648 | tf_op jit(solution)/shard_map/ppermute | solution.py:235
  17.7 0.8 %shard_map.53 = (f32[24,40,128]{2,1,0:T(8,128)S(1)}, f32[24,40,128]{2,1,0:T(8,128)S(1)}, f32[24,40,128]{2,1,0:T(8,128)S(1)}, f32[24,40,128]{2,1,0:T(8,128)S(1)},...) custom-call(f32[16,32,128]{2,1,0:T(8,128)S(1)} %copy-done.1, ...), custom_call_target="tpu_custom_call" | custom-call | tf_op jit(solution)/shard_map/pallas_call | solution.py:623
  18.5 3.0 %collective-permute-done.4.ya2 = f32[240,128]{1,0:T(8,128)S(1)} collective-permute-done((f32[240,128]{1,0:T(8,128)S(1)}, f32[240,128]{1,0:T(8,128)S(1)}, u32[]{:S(2)}, u32[]{:S(2)}) %collective-permute-start.4) | collective-permute-done | bytes 122912 | tf_op jit(solution)/shard_map/ppermute | solution.py:235
  21.6 0.9 %shard_map.54 = (f32[16,8,128]{2,1,0:T(8,128)S(1)}, f32[3,8,24,128]{3,2,1,0:T(8,128)S(1)}, f32[344,128]{1,0:T(8,128)S(1)}, f32[344,128]{1,0:T(8,128)S(1)}, f32[64,128]{1,0:T(8,128)S(1)}, /*index=5*/f32[64,128]{1,0:T(8,128)S(1)}) custom-call(f32[16,32,128]{2,1,0:T(8,128)S(1)} %copy-done.1, f32[16,32,128]{2,1,0:T(8,128)S(1)} %copy-done, ...), custom_call_target="tpu_custom_call" | custom-call | tf_op jit(solution)/shard_map/pallas_call | solution.py:623
  22.5 0.1 collective-permute-start.6
  22.6 3.2 %collective-permute-start.7 = (f32[344,128]{1,0:T(8,128)S(1)}, f32[344,128]{1,0:T(8,128)S(1)}, u32[]{:S(2)}, u32[]{:S(2)}) collective-permute-start(f32[344,128]{1,0:T(8,128)S(1)} %get-tuple-element.108), channel_id=1, source_target_pairs={{0,1},{1,0},{2,3},{3,2},{4,5},{5,4},{6,7},{7,6},{8,16},{9,17},{10,... | collective-permute-start | bytes 528392 | tf_op jit(solution)/shard_map/ppermute | solution.py:235
  25.8 1.5 %collective-permute-start.8 = (f32[64,128]{1,0:T(8,128)S(1)}, f32[64,128]{1,0:T(8,128)S(1)}, u32[]{:S(2)}, u32[]{:S(2)}) collective-permute-start(f32[64,128]{1,0:T(8,128)S(1)} %get-tuple-element.109), channel_id=1, source_target_pairs={{0,1},{1,0},{2,3},{3,2},{4,5},{5,4},{6,7},{7,6},{8,9},{9,8},{10,11... | collective-permute-start | bytes 98312 | tf_op jit(solution)/shard_map/ppermute | solution.py:235
  27.3 0.4 %collective-permute-start.9 = (f32[64,128]{1,0:T(8,128)S(1)}, f32[64,128]{1,0:T(8,128)S(1)}, u32[]{:S(2)}, u32[]{:S(2)}) collective-permute-start(f32[64,128]{1,0:T(8,128)S(1)} %get-tuple-element.110), channel_id=1, source_target_pairs={{0,16},{1,17},{2,18},{3,19},{4,20},{5,21},{6,22},{7,23},{8,24},{9,... | collective-permute-start | bytes 98312 | tf_op jit(solution)/shard_map/ppermute | solution.py:235
  27.7 0.9 %collective-permute-done.6.near_a = f32[344,128]{1,0:T(8,128)S(1)} collective-permute-done((f32[344,128]{1,0:T(8,128)S(1)}, f32[344,128]{1,0:T(8,128)S(1)}, u32[]{:S(2)}, u32[]{:S(2)}) %collective-permute-start.6) | collective-permute-done | bytes 176160 | tf_op jit(solution)/shard_map/ppermute | solution.py:235
  28.6 2.6 %collective-permute-done.7.near_b = f32[344,128]{1,0:T(8,128)S(1)} collective-permute-done((f32[344,128]{1,0:T(8,128)S(1)}, f32[344,128]{1,0:T(8,128)S(1)}, u32[]{:S(2)}, u32[]{:S(2)}) %collective-permute-start.7) | collective-permute-done | bytes 176160 | tf_op jit(solution)/shard_map/ppermute | solution.py:235
  31.2 1.4 %shard_map.55 = (f32[14,40,128]{2,1,0:T(8,128)S(1)}, f32[14,40,128]{2,1,0:T(8,128)S(1)}, f32[14,40,128]{2,1,0:T(8,128)S(1)}, f32[14,40,128]{2,1,0:T(8,128)S(1)},...) custom-call(f32[3,8,24,128]{3,2,1,0:T(8,128)S(1)} %get-tuple-element, ...), custom_call_target="tpu_custom_call" | custom-call | tf_op jit(solution)/shard_map/pallas_call | solution.py:623
  32.5 0.2 collective-permute-done.8.far_a
  32.7 1.5 %shard_map.56 = (f32[16,32,128]{2,1,0:T(8,128)}, f32[8,16,64]{2,1,0:T(8,128)}) custom-call(f32[16,32,128]{2,1,0:T(8,128)S(1)} %get-tuple-element.86.x_fine, f32[16,8,128]{2,1,0:T(8,128)S(1)} %get-tuple-element.105.x_edge, f32[3,8,24,128]{3,2,1,0:T(8,128)S(1)} %get-tuple-element.106.ext, f32[344,128]{1,0:T(8,128)S(1)} %collective-permute-done.6.near_a, ...), custom_call_target="tpu_custom_call" | custom-call | tf_op jit(solution)/shard_map/pallas_call | solution.py:623
  (14 shorter events, 0.1 us)
Async XLA Ops:
  0.6 1.0 %copy-start.2 = (f32[16,32,128]{2,1,0:T(8,128)S(1)}, f32[16,32,128]{2,1,0:T(8,128)}, u32[]{:S(2)}) copy-start(f32[16,32,128]{2,1,0:T(8,128)} %shift.9) | copy-start | bytes 786436
  0.6 1.1 %copy-start = (f32[16,32,128]{2,1,0:T(8,128)S(1)}, f32[16,32,128]{2,1,0:T(8,128)}, u32[]{:S(2)}) copy-start(f32[16,32,128]{2,1,0:T(8,128)} %beta.9) | copy-start | bytes 786436
  1.8 7.2 %copy-start.1 = (f32[16,32,128]{2,1,0:T(8,128)S(1)}, f32[16,32,128]{2,1,0:T(8,128)}, u32[]{:S(2)}) copy-start(f32[16,32,128]{2,1,0:T(8,128)} %b.9) | copy-start | bytes 786436
  1.8 13.9 %collective-permute-start.1 = (f32[13,32,128]{2,1,0:T(8,128)S(1)}, f32[13,32,128]{2,1,0:T(8,128)S(1)}, u32[]{:S(2)}, u32[]{:S(2)}) collective-permute-start(f32[13,32,128]{2,1,0:T(8,128)S(1)} %get-tuple-element.132), channel_id=1, source_target_pairs={{0,8},{1,9},{2,10},{3,11},{4,12},{5,13},{6,14},{7,15},{8,0},{9,1},... | collective-permute-start | bytes 638984 | tf_op jit(solution)/shard_map/ppermute | solution.py:235
  3.8 11.9 %collective-permute-start = (f32[13,32,128]{2,1,0:T(8,128)S(1)}, f32[13,32,128]{2,1,0:T(8,128)S(1)}, u32[]{:S(2)}, u32[]{:S(2)}) collective-permute-start(f32[13,32,128]{2,1,0:T(8,128)S(1)} %get-tuple-element.133), channel_id=1, source_target_pairs={{0,1},{1,0},{2,3},{3,2},{4,5},{5,4},{6,7},{7,6},{8,16},{9,17},{10,... | collective-permute-start | bytes 638984 | tf_op jit(solution)/shard_map/ppermute | solution.py:235
  9.1 5.8 %collective-permute-start.2 = (f32[400,128]{1,0:T(8,128)S(1)}, f32[400,128]{1,0:T(8,128)S(1)}, u32[]{:S(2)}, u32[]{:S(2)}) collective-permute-start(f32[400,128]{1,0:T(8,128)S(1)} %get-tuple-element.70), channel_id=1, source_target_pairs={{0,8},{1,2},{2,1},{3,4},{4,3},{5,6},{6,5},{7,15},{8,0},{9,10},{10,... | collective-permute-start | bytes 614408 | tf_op jit(solution)/shard_map/ppermute | solution.py:235
  9.2 5.7 %collective-permute-start.3 = (f32[400,128]{1,0:T(8,128)S(1)}, f32[400,128]{1,0:T(8,128)S(1)}, u32[]{:S(2)}, u32[]{:S(2)}) collective-permute-start(f32[400,128]{1,0:T(8,128)S(1)} %get-tuple-element.71), channel_id=1, source_target_pairs={{0,1},{1,0},{2,3},{3,2},{4,5},{5,4},{6,7},{7,6},{8,9},{9,8},{10,11... | collective-permute-start | bytes 614408 | tf_op jit(solution)/shard_map/ppermute | solution.py:235
  16.6 5.0 %collective-permute-start.4 = (f32[240,128]{1,0:T(8,128)S(1)}, f32[240,128]{1,0:T(8,128)S(1)}, u32[]{:S(2)}, u32[]{:S(2)}) collective-permute-start(f32[240,128]{1,0:T(8,128)S(1)} %get-tuple-element.88), channel_id=1, source_target_pairs={{0,8},{1,2},{2,1},{3,4},{4,3},{5,6},{6,5},{7,15},{8,0},{9,10},{10,... | collective-permute-start | bytes 368648 | tf_op jit(solution)/shard_map/ppermute | solution.py:235
  16.7 4.9 %collective-permute-start.5 = (f32[240,128]{1,0:T(8,128)S(1)}, f32[240,128]{1,0:T(8,128)S(1)}, u32[]{:S(2)}, u32[]{:S(2)}) collective-permute-start(f32[240,128]{1,0:T(8,128)S(1)} %get-tuple-element.89), channel_id=1, source_target_pairs={{0,1},{1,0},{2,3},{3,2},{4,5},{5,4},{6,7},{7,6},{8,9},{9,8},{10,11... | collective-permute-start | bytes 368648 | tf_op jit(solution)/shard_map/ppermute | solution.py:235
  22.5 6.1 %collective-permute-start.6 = (f32[344,128]{1,0:T(8,128)S(1)}, f32[344,128]{1,0:T(8,128)S(1)}, u32[]{:S(2)}, u32[]{:S(2)}) collective-permute-start(f32[344,128]{1,0:T(8,128)S(1)} %get-tuple-element.107), channel_id=1, source_target_pairs={{0,8},{1,9},{2,10},{3,11},{4,12},{5,13},{6,14},{7,15},{8,0},{9,1},... | collective-permute-start | bytes 528392 | tf_op jit(solution)/shard_map/ppermute | solution.py:235
  22.6 8.6 %collective-permute-start.7 = (f32[344,128]{1,0:T(8,128)S(1)}, f32[344,128]{1,0:T(8,128)S(1)}, u32[]{:S(2)}, u32[]{:S(2)}) collective-permute-start(f32[344,128]{1,0:T(8,128)S(1)} %get-tuple-element.108), channel_id=1, source_target_pairs={{0,1},{1,0},{2,3},{3,2},{4,5},{5,4},{6,7},{7,6},{8,16},{9,17},{10,... | collective-permute-start | bytes 528392 | tf_op jit(solution)/shard_map/ppermute | solution.py:235
  25.8 6.9 %collective-permute-start.8 = (f32[64,128]{1,0:T(8,128)S(1)}, f32[64,128]{1,0:T(8,128)S(1)}, u32[]{:S(2)}, u32[]{:S(2)}) collective-permute-start(f32[64,128]{1,0:T(8,128)S(1)} %get-tuple-element.109), channel_id=1, source_target_pairs={{0,1},{1,0},{2,3},{3,2},{4,5},{5,4},{6,7},{7,6},{8,9},{9,8},{10,11... | collective-permute-start | bytes 98312 | tf_op jit(solution)/shard_map/ppermute | solution.py:235
  27.3 5.5 %collective-permute-start.9 = (f32[64,128]{1,0:T(8,128)S(1)}, f32[64,128]{1,0:T(8,128)S(1)}, u32[]{:S(2)}, u32[]{:S(2)}) collective-permute-start(f32[64,128]{1,0:T(8,128)S(1)} %get-tuple-element.110), channel_id=1, source_target_pairs={{0,16},{1,17},{2,18},{3,19},{4,20},{5,21},{6,22},{7,23},{8,24},{9,... | collective-permute-start | bytes 98312 | tf_op jit(solution)/shard_map/ppermute | solution.py:235
where the time goes:
time: 34.3 us; the launch traced here: 34.2 us
  starting transfers between devices  15.1 us (44%)
  waiting for transfers between devices  10.9 us (32%)
  Pallas kernels  6.33 us (18%)
  local copies, waits for them, and re-layouts  1.07 us (3%)
  between operations  0.78 us (2%)
    ppermute x5, waiting for transfers between devices, swaps(): lax.ppermute(first, axes, orders[0])  8.3 us
    ppermute x5, starting transfers between devices, swaps(): lax.ppermute(second, axes, orders[1])  8.21 us
    ppermute x5, starting transfers between devices, swaps(): lax.ppermute(first, axes, orders[0])  6.85 us
    pallas_call x7, Pallas kernels, call(): pl.pallas_call(kernel, out_shape=[jax.ShapeDtypeStruct(s, F32) for s in o...  6.33 us
    ppermute x5, waiting for transfers between devices, swaps(): lax.ppermute(second, axes, orders[1])  2.61 us
    slice x3, local copies, waits for them, and re-layouts, pack_fine_x(): f[16 - n:]  0.96 us
  transfers between devices with their start and end apart: 10, of which 5 were waited for; matrix products, arithmetic and copies ran while one was open for 0% of the time, Pallas kernels for 9%

commit v1 on v0

--- a/solution.py
+++ b/solution.py
@@ -69,16 +69,16 @@
     return jnp.where(lanes(value.shape[0]) % 2 == 0, roll(value, -1), roll(value, 1))
 
 
-def build(level, scale, beta, rhs, shift, work, planes=None):
+def build(level, beta, rhs, shift, work, planes=None):
     wx, wy, wym, wz, wzm, diag, inv, rhs_n, start = work
-    rep, half, last_span = level.rep, 0.5 * scale, None
+    rep, last_span = level.rep, None
     planes = range(level.planes) if planes is None else planes
     for base, i in [(base, i) for base in level.bases for i in planes]:
         lo, n = level.span(i, level.depth)
         lo += base
         if (lo, n, i) != last_span:
             prev, cur = beta[i, pl.ds(8 + lo, n), :], beta[i + 1, pl.ds(8 + lo, n), :]
-            wx_prev = half * (prev + cur)
+            wx_prev = prev + cur
             if i:
                 wx[i - 1, pl.ds(lo, n), :] = wx_prev
             lane = lanes(n)
@@ -86,11 +86,11 @@
         last_span = (lo, n, i + 1)
         at = pl.ds(lo, n)
         nxt = beta[i + 2, pl.ds(8 + lo, n), :]
-        wx_next = half * (cur + nxt)
-        w_up = half * (cur + beta[i + 1, pl.ds(9 + lo, n), :])
-        w_down = half * (cur + beta[i + 1, pl.ds(7 + lo, n), :])
-        w_right = half * (cur + jnp.where(last, 0.0, roll(cur, -rep)))
-        w_left = half * (cur + jnp.where(first, 0.0, roll(cur, rep)))
+        wx_next = cur + nxt
+        w_up = cur + beta[i + 1, pl.ds(9 + lo, n), :]
+        w_down = cur + beta[i + 1, pl.ds(7 + lo, n), :]
+        w_right = cur + jnp.where(last, 0.0, roll(cur, -rep))
+        w_left = cur + jnp.where(first, 0.0, roll(cur, rep))
         d = shift(i, at) + (wx_prev + wx_next + w_up + w_down + w_right + w_left)
         iv = jnp.where(cur > 0.0, 1.0 / d, 0.0)
         wx[i, at, :] = wx_next
@@ -265,13 +265,8 @@
     out_b[pl.ds(at, count), :] = jnp.where(up, lower, higher)
 
 
-def pack_face_y(b, beta, shift, out_a, out_b, packed, pair):
+def pack_face_y(b, beta, shift, out_a, out_b):
     up = upward("gy", 1)
-    for field, src in ((1, beta), (2, shift)):
-        for m in range(8):
-            at = 8 * field + m - 8
-            pair[at] = src[2 * m] + src[2 * m + 1]
-            packed[field - 1, m] = pack_pairs(pair, at, 0, 8)
     for field, src in enumerate((b, beta, shift)):
         for x in range(16):
             n = FACE_Y[field, x][1]
@@ -323,19 +318,24 @@
 def edge_rows(be, x, beta, ya_in, yb_in):
     (low, high), up = y_flags(), upward("gy", 1)
     lo, hi = y_sides(FACE_Y, (1, x), ya_in, yb_in, up)
-    be[x + 5, 8:40, :] = beta[x]
-    be[x + 5, 7:8, :] = lo[8:9] * low
-    be[x + 5, 40:41, :] = hi[0:1] * high
+    be[x + 5, 8:40, :] = beta[x] * 0.5
+    be[x + 5, 7:8, :] = lo[8:9] * (0.5 * low)
+    be[x + 5, 40:41, :] = hi[0:1] * (0.5 * high)
 
 
 def inner_kernel(
     b, beta, shift, ya_in, yb_in,
-    wx, wy, wym, wz, wzm, diag, inv, rhs_n, x0, x1, x2, x3, step, pair, be,
+    wx, wy, wym, wz, wzm, diag, inv, rhs_n, x0, x1, x2, x3, step, pair, packed, be, sums,
 ):
+    for field, src in ((1, beta), (2, shift)):
+        for m in range(8):
+            at = 8 * field + m - 8
+            sums[at] = src[2 * m] + src[2 * m + 1]
+            packed[field - 1, m] = pack_pairs(sums, at, 0, 8)
     for x in range(16):
         edge_rows(be, x, beta, ya_in, yb_in)
     work = (wx, wy, wym, wz, wzm, diag, inv, rhs_n, x0)
-    build(FINE, 1.0, be, lambda i, at: b[i - 4], lambda i, at: shift[i - 4], work, INNER(0))
+    build(FINE, be, lambda i, at: b[i - 4], lambda i, at: shift[i - 4], work, INNER(0))
     sweeps(FINE, work, (x0, x1, x2, x3), step, INNER)
     pair_residual(FINE, x3, work, pair, 0, range(10, 14))
 
@@ -352,7 +352,7 @@
             edge_rows(be, x, beta, ya_in, yb_in)
             continue
         p = fine_plane(1, x, own, xa_in, xb_in, up_x)
-        be[x + 5, 8:40, :] = p * (near[-1] if x < 0 else near[1])
+        be[x + 5, 8:40, :] = p * (0.5 * (near[-1] if x < 0 else near[1]))
         at = SECOND_Y[1, "fine", x][1]
         put_both(out_a, out_b, SECOND_Y, (1, "fine", x), up_y, p[32 - at:32], p[0:at])
     for field, dst in ((0, bb), (2, ss)):
@@ -366,7 +366,7 @@
     def plane_of(src, halo):
         return lambda i, at: src[i - 4] if 4 <= i < 20 else halo[i]
 
-    build(FINE, 1.0, be, plane_of(b, bb), plane_of(shift, ss), work, rest(0))
+    build(FINE, be, plane_of(b, bb), plane_of(shift, ss), work, rest(0))
     x = sweeps(FINE, work, fields, step, rest)
     pair_residual(FINE, x, work, pair, 0, [*range(4, 10), *range(14, 20)])
     for m in range(8):
@@ -387,10 +387,10 @@
     (low, high), up_y = y_flags(), upward("gy", 1)
     for x in range(16):
         lo, hi = y_sides(FACE_Y, (1, x), ya_in, yb_in, up_y)
-        be[x + 5, 16:25, :] = beta[x, 0:9, :]
-        be[x + 5, 31:40, :] = beta[x, 23:32, :]
-        be[x + 5, 7:16, :] = lo * low
-        be[x + 5, 40:49, :] = hi * high
+        be[x + 5, 16:25, :] = beta[x, 0:9, :] * 0.5
+        be[x + 5, 31:40, :] = beta[x, 23:32, :] * 0.5
+        be[x + 5, 7:16, :] = lo * (0.5 * low)
+        be[x + 5, 40:49, :] = hi * (0.5 * high)
     for field, src, dst in ((0, b, bb), (2, shift, ss)):
         for x in range(16):
             lo, hi = y_sides(FACE_Y, (field, x), ya_in, yb_in, up_y)
@@ -399,12 +399,12 @@
             dst[x + 4, 0:8, :] = lo
             dst[x + 4, 32:40, :] = hi
     work = (wx, wy, wym, wz, wzm, diag, inv, rhs_n, x0)
-    build(STRIP, 1.0, be, lambda i, at: bb[i, at, :], lambda i, at: ss[i, at, :], work, INNER(0))
+    build(STRIP, be, lambda i, at: bb[i, at, :], lambda i, at: ss[i, at, :], work, INNER(0))
     sweeps(STRIP, work, (x0, x1, x2, x3), step, INNER)
     pair_residual(STRIP, x3, work, pair, 0, range(10, 14))
 
     for m in range(8):
-        sums[m] = be[2 * m + 5] + be[2 * m + 6]
+        sums[m] = (be[2 * m + 5] + be[2 * m + 6]) * 2.0
         sums[m + 8, 0:40, :] = ss[2 * m + 4] + ss[2 * m + 5]
         for field, plane, at in ((1, m, 8), (2, m + 8, 0)):
             dst = ext.at[field - 1, m]
@@ -431,9 +431,8 @@
         p = fine_plane(1, x, own, xa_in, xb_in, up_x)
         lo, hi = sides(1, x)
         n = lo.shape[0]
-        f = 1.0 if 0 <= x < 16 else near[-1] if x < 0 else near[1]
-        if not 0 <= x < 16:
-            p = p * f
+        f = 0.5 if 0 <= x < 16 else 0.5 * (near[-1] if x < 0 else near[1])
+        p = p * f
         be[x + 5, 16:25, :] = p[0:9]
         be[x + 5, 31:40, :] = p[23:32]
         be[x + 5, pl.ds(16 - n, n), :] = lo * (low * f)
@@ -448,7 +447,7 @@
             dst[x + 4, pl.ds(8 - n, n), :] = lo
             dst[x + 4, pl.ds(32, n), :] = hi
     work, fields, step, pair = split_work(inner, outer, STRIP)
-    build(STRIP, 1.0, be, lambda i, at: bb[i, at, :], lambda i, at: ss[i, at, :], work, rest(0))
+    build(STRIP, be, lambda i, at: bb[i, at, :], lambda i, at: ss[i, at, :], work, rest(0))
     x = sweeps(STRIP, work, fields, step, rest)
     pair_residual(STRIP, x, work, pair, 0, [*range(4, 10), *range(14, 20)])
     for m in range(8):
@@ -487,14 +486,15 @@
     if d <= 0:
         n = side_rows(field, 0)
         at = pl.ds(6 - n, 8 + 2 * n)
-        return ext[field, -d, at, :], ext[field, 7 + d, at, :]
+        lower, higher = ext[field, -d, at, :], ext[field, 7 + d, at, :]
+        return (lower * 0.125, higher * 0.125) if field == 1 else (lower, higher)
     hop, rows, (a, c) = (1, NEAR_X, near) if d <= 8 else (2, FAR_X, far)
     u = upward("gx", hop, 2 - hop)
     a, c = pick(a, rows, (field, d)), pick(c, rows, (field, d))
     lower, higher = jnp.where(u, c, a), jnp.where(u, a, c)
     if field == 1:
         flags = x_flags()
-        return lower * flags[-hop], higher * flags[hop]
+        return lower * (0.125 * flags[-hop]), higher * (0.125 * flags[hop])
     return lower, higher
 
 
@@ -542,7 +542,7 @@
     unpack_mid(2, range(3, 14), ss, 12, 10, *messages)
     be[15, pl.ds(8, 40), :] = swap_lanes(be[14, pl.ds(8, 40), :])
     work = (wx, wy, wym, wz, wzm, diag, inv, rhs_n, x0)
-    build(MID, 0.25, be, lambda i, at: bb[i, at, :], lambda i, at: ss[i, at, :], work, MID_INNER(0))
+    build(MID, be, lambda i, at: bb[i, at, :], lambda i, at: ss[i, at, :], work, MID_INNER(0))
     sweeps(MID, work, (x0, x1, x2, x3), step, MID_INNER)
     pair_mid_residual(x3, work, pair, range(8, 14))
 
@@ -551,12 +551,12 @@
     for m in range(5):
         sums[6 + m] = ss[2 * m + 4] + ss[2 * m + 5]
     for m in range(6):
-        be2[m, 8:24, :] = down_sample(sums, m)
+        be2[m, 8:24, :] = down_sample(sums, m) * 0.25
     be2[6, 8:24, :] = swap_lanes(be2[5, 8:24, :])
     for m in range(5):
         ss2[m] = down_sample(sums, 6 + m)
     work2 = (wx2, wy2, wym2, wz2, wzm2, diag2, inv2, None, None)
-    build(LOW, 0.0625, be2, None, lambda i, at: ss2[i, at, :], work2)
+    build(LOW, be2, None, lambda i, at: ss2[i, at, :], work2)
 
 
 def coarse_kernel(
@@ -579,7 +579,7 @@
     def rest(k):
         return range(k, 3 + k)
 
-    build(MID, 0.25, be, lambda i, at: bb[i, at, :], lambda i, at: ss[i, at, :], work, rest(0))
+    build(MID, be, lambda i, at: bb[i, at, :], lambda i, at: ss[i, at, :], work, rest(0))
     x1 = sweeps(MID, work, fields, StepSplit(i_step, step, MID_INNER(1), MID), rest)
     pair = Split(i_pair, pair, 2, 4)
     pair_mid_residual(x1, work, pair, range(4, 8))
@@ -647,11 +647,14 @@
     fields = (b, beta, shift)
     a, c = pack_fine_x(fields)
     xs = swaps(a, c, "gx", 1)
-    a, c, packed_c = call(
-        pack_face_y, fields, [(FACE_Y_SIZE, 128)] * 2 + [(2, 8, 8, 128)], [vmem(16, 32, 128)]
+    a, c = call(pack_face_y, fields, [(FACE_Y_SIZE, 128)] * 2)
+    ys = swaps(a, c, "gy", 1)
+    *inner, packed_c = call(
+        inner_kernel,
+        (*fields, *ys),
+        work_shapes(24, 32, 8) + [(2, 8, 8, 128)],
+        [vmem(26, 48, 128), vmem(16, 32, 128)],
     )
-    ys = swaps(a, c, "gy", 1)
-    inner = call(inner_kernel, (*fields, *ys), work_shapes(24, 32, 8), [vmem(26, 48, 128)])
     x_fine, packed, a, c = call(
         outer_kernel,
         (*fields, packed_c, *xs, *ys, *inner),

time: 34.3 us -> 34.3 us (level)
  no operation moved by 1% of the time
where the time goes in v1:
time: 34.3 us; the launch traced here: 34.2 us
  starting transfers between devices  15.1 us (44%)
  waiting for transfers between devices  11 us (32%)
  Pallas kernels  6.25 us (18%)
  local copies, waits for them, and re-layouts  1.07 us (3%)
  between operations  0.78 us (2%)
    ppermute x5, waiting for transfers between devices, swaps(): lax.ppermute(first, axes, orders[0])  8.37 us
    ppermute x5, starting transfers between devices, swaps(): lax.ppermute(second, axes, orders[1])  8.21 us
    ppermute x5, starting transfers between devices, swaps(): lax.ppermute(first, axes, orders[0])  6.85 us
    pallas_call x7, Pallas kernels, call(): pl.pallas_call(kernel, out_shape=[jax.ShapeDtypeStruct(s, F32) for s in o...  6.25 us
    ppermute x5, waiting for transfers between devices, swaps(): lax.ppermute(second, axes, orders[1])  2.61 us
    slice x3, local copies, waits for them, and re-layouts, pack_fine_x(): f[16 - n:]  0.96 us
  transfers between devices with their start and end apart: 10, of which 5 were waited for; matrix products, arithmetic and copies ran while one was open for 0% of the time, Pallas kernels for 9%

profile of v1, /device:TPU:24, one launch (start us, length us, event | category | flops | bytes accessed | tf_op | source)
XLA Modules:
  0.0 34.2 jit_solution(14937364984969849453)
XLA Ops:
  0.7 0.9 %fusion = (f32[4,32,128]{2,1,0:T(8,128)S(1)}, f32[4,32,128]{2,1,0:T(8,128)S(1)}) fusion(f32[16,32,128]{2,1,0:T(8,128)} %b.9), kind=kLoop, calls=%fused_computation.4 | loop fusion | bytes 262144 | tf_op jit(solution)/shard_map/slice | solution.py:243
  1.6 0.1 copy-done
  1.8 0.0 copy-start.1
  1.8 2.0 %collective-permute-start.3 = (f32[13,32,128]{2,1,0:T(8,128)S(1)}, f32[13,32,128]{2,1,0:T(8,128)S(1)}, u32[]{:S(2)}, u32[]{:S(2)}) collective-permute-start(f32[13,32,128]{2,1,0:T(8,128)S(1)} %get-tuple-element.132), channel_id=1, source_target_pairs={{0,8},{1,9},{2,10},{3,11},{4,12},{5,13},{6,14},{7,15},{8,0},{9,1},... | collective-permute-start | bytes 638984 | tf_op jit(solution)/shard_map/ppermute | solution.py:235
  3.8 5.1 %collective-permute-start.2 = (f32[13,32,128]{2,1,0:T(8,128)S(1)}, f32[13,32,128]{2,1,0:T(8,128)S(1)}, u32[]{:S(2)}, u32[]{:S(2)}) collective-permute-start(f32[13,32,128]{2,1,0:T(8,128)S(1)} %get-tuple-element.133), channel_id=1, source_target_pairs={{0,1},{1,0},{2,3},{3,2},{4,5},{5,4},{6,7},{7,6},{8,16},{9,17},{10,... | collective-permute-start | bytes 638984 | tf_op jit(solution)/shard_map/ppermute | solution.py:235
  9.0 0.1 collective-permute-start
  9.1 1.6 %collective-permute-start.1 = (f32[400,128]{1,0:T(8,128)S(1)}, f32[400,128]{1,0:T(8,128)S(1)}, u32[]{:S(2)}, u32[]{:S(2)}) collective-permute-start(f32[400,128]{1,0:T(8,128)S(1)} %get-tuple-element.68), channel_id=1, source_target_pairs={{0,1},{1,0},{2,3},{3,2},{4,5},{5,4},{6,7},{7,6},{8,9},{9,8},{10,11... | collective-permute-start | bytes 614408 | tf_op jit(solution)/shard_map/ppermute | solution.py:235
  10.7 4.2 %collective-permute-done.ya_in = f32[400,128]{1,0:T(8,128)S(1)} collective-permute-done((f32[400,128]{1,0:T(8,128)S(1)}, f32[400,128]{1,0:T(8,128)S(1)}, u32[]{:S(2)}, u32[]{:S(2)}) %collective-permute-start) | collective-permute-done | bytes 204832 | tf_op jit(solution)/shard_map/ppermute | solution.py:235
  14.9 0.8 %shard_map.51 = (f32[24,32,128]{2,1,0:T(8,128)S(1)}, f32[24,32,128]{2,1,0:T(8,128)S(1)}, f32[24,32,128]{2,1,0:T(8,128)S(1)}, f32[24,32,128]{2,1,0:T(8,128)S(1)},...) custom-call(f32[16,32,128]{2,1,0:T(8,128)S(1)} %copy-done.1, ...), custom_call_target="tpu_custom_call" | custom-call | tf_op jit(solution)/shard_map/pallas_call | solution.py:623
  15.7 0.9 %shard_map.52 = (f32[16,32,128]{2,1,0:T(8,128)S(1)}, f32[8,8,128]{2,1,0:T(8,128)S(1)}, f32[240,128]{1,0:T(8,128)S(1)}, f32[240,128]{1,0:T(8,128)S(1)}) custom-call(f32[16,32,128]{2,1,0:T(8,128)S(1)} %copy-done.1, f32[16,32,128]{2,1,0:T(8,128)S(1)} %copy-done, f32[16,32,128]{2,1,0:T(8,128)S(1)} %copy-done.2, ...), custom_call_target="tpu_custom_call" | custom-call | tf_op jit(solution)/shard_map/pallas_call | solution.py:623
  16.6 0.1 collective-permute-start.4
  16.6 1.0 %collective-permute-start.5 = (f32[240,128]{1,0:T(8,128)S(1)}, f32[240,128]{1,0:T(8,128)S(1)}, u32[]{:S(2)}, u32[]{:S(2)}) collective-permute-start(f32[240,128]{1,0:T(8,128)S(1)} %get-tuple-element.89), channel_id=1, source_target_pairs={{0,1},{1,0},{2,3},{3,2},{4,5},{5,4},{6,7},{7,6},{8,9},{9,8},{10,11... | collective-permute-start | bytes 368648 | tf_op jit(solution)/shard_map/ppermute | solution.py:235
  17.7 0.8 %shard_map.53 = (f32[24,40,128]{2,1,0:T(8,128)S(1)}, f32[24,40,128]{2,1,0:T(8,128)S(1)}, f32[24,40,128]{2,1,0:T(8,128)S(1)}, f32[24,40,128]{2,1,0:T(8,128)S(1)},...) custom-call(f32[16,32,128]{2,1,0:T(8,128)S(1)} %copy-done.1, ...), custom_call_target="tpu_custom_call" | custom-call | tf_op jit(solution)/shard_map/pallas_call | solution.py:623
  18.5 3.0 %collective-permute-done.4.ya2 = f32[240,128]{1,0:T(8,128)S(1)} collective-permute-done((f32[240,128]{1,0:T(8,128)S(1)}, f32[240,128]{1,0:T(8,128)S(1)}, u32[]{:S(2)}, u32[]{:S(2)}) %collective-permute-start.4) | collective-permute-done | bytes 122912 | tf_op jit(solution)/shard_map/ppermute | solution.py:235
  21.5 0.9 %shard_map.54 = (f32[16,8,128]{2,1,0:T(8,128)S(1)}, f32[3,8,24,128]{3,2,1,0:T(8,128)S(1)}, f32[344,128]{1,0:T(8,128)S(1)}, f32[344,128]{1,0:T(8,128)S(1)}, f32[64,128]{1,0:T(8,128)S(1)}, /*index=5*/f32[64,128]{1,0:T(8,128)S(1)}) custom-call(f32[16,32,128]{2,1,0:T(8,128)S(1)} %copy-done.1, f32[16,32,128]{2,1,0:T(8,128)S(1)} %copy-done, ...), custom_call_target="tpu_custom_call" | custom-call | tf_op jit(solution)/shard_map/pallas_call | solution.py:623
  22.4 0.1 collective-permute-start.6
  22.5 3.3 %collective-permute-start.7 = (f32[344,128]{1,0:T(8,128)S(1)}, f32[344,128]{1,0:T(8,128)S(1)}, u32[]{:S(2)}, u32[]{:S(2)}) collective-permute-start(f32[344,128]{1,0:T(8,128)S(1)} %get-tuple-element.108), channel_id=1, source_target_pairs={{0,1},{1,0},{2,3},{3,2},{4,5},{5,4},{6,7},{7,6},{8,16},{9,17},{10,... | collective-permute-start | bytes 528392 | tf_op jit(solution)/shard_map/ppermute | solution.py:235
  25.8 1.5 %collective-permute-start.8 = (f32[64,128]{1,0:T(8,128)S(1)}, f32[64,128]{1,0:T(8,128)S(1)}, u32[]{:S(2)}, u32[]{:S(2)}) collective-permute-start(f32[64,128]{1,0:T(8,128)S(1)} %get-tuple-element.109), channel_id=1, source_target_pairs={{0,1},{1,0},{2,3},{3,2},{4,5},{5,4},{6,7},{7,6},{8,9},{9,8},{10,11... | collective-permute-start | bytes 98312 | tf_op jit(solution)/shard_map/ppermute | solution.py:235
  27.2 0.3 collective-permute-start.9
  27.6 0.9 %collective-permute-done.6.near_a = f32[344,128]{1,0:T(8,128)S(1)} collective-permute-done((f32[344,128]{1,0:T(8,128)S(1)}, f32[344,128]{1,0:T(8,128)S(1)}, u32[]{:S(2)}, u32[]{:S(2)}) %collective-permute-start.6) | collective-permute-done | bytes 176160 | tf_op jit(solution)/shard_map/ppermute | solution.py:235
  28.5 2.6 %collective-permute-done.7.near_b = f32[344,128]{1,0:T(8,128)S(1)} collective-permute-done((f32[344,128]{1,0:T(8,128)S(1)}, f32[344,128]{1,0:T(8,128)S(1)}, u32[]{:S(2)}, u32[]{:S(2)}) %collective-permute-start.7) | collective-permute-done | bytes 176160 | tf_op jit(solution)/shard_map/ppermute | solution.py:235
  31.1 1.4 %shard_map.55 = (f32[14,40,128]{2,1,0:T(8,128)S(1)}, f32[14,40,128]{2,1,0:T(8,128)S(1)}, f32[14,40,128]{2,1,0:T(8,128)S(1)}, f32[14,40,128]{2,1,0:T(8,128)S(1)},...) custom-call(f32[3,8,24,128]{3,2,1,0:T(8,128)S(1)} %get-tuple-element, ...), custom_call_target="tpu_custom_call" | custom-call | tf_op jit(solution)/shard_map/pallas_call | solution.py:623
  32.5 0.3 collective-permute-done.8.far_a
  32.7 1.5 %shard_map.56 = (f32[16,32,128]{2,1,0:T(8,128)}, f32[8,16,64]{2,1,0:T(8,128)}) custom-call(f32[16,32,128]{2,1,0:T(8,128)S(1)} %get-tuple-element.86.x_fine, f32[16,8,128]{2,1,0:T(8,128)S(1)} %get-tuple-element.105.x_edge, f32[3,8,24,128]{3,2,1,0:T(8,128)S(1)} %get-tuple-element.106.ext, f32[344,128]{1,0:T(8,128)S(1)} %collective-permute-done.6.near_a, ...), custom_call_target="tpu_custom_call" | custom-call | tf_op jit(solution)/shard_map/pallas_call | solution.py:623
  (14 shorter events, 0.2 us)
Async XLA Ops:
  0.6 1.0 %copy-start.2 = (f32[16,32,128]{2,1,0:T(8,128)S(1)}, f32[16,32,128]{2,1,0:T(8,128)}, u32[]{:S(2)}) copy-start(f32[16,32,128]{2,1,0:T(8,128)} %shift.9) | copy-start | bytes 786436
  0.6 1.1 %copy-start = (f32[16,32,128]{2,1,0:T(8,128)S(1)}, f32[16,32,128]{2,1,0:T(8,128)}, u32[]{:S(2)}) copy-start(f32[16,32,128]{2,1,0:T(8,128)} %beta.9) | copy-start | bytes 786436
  1.8 7.2 %copy-start.1 = (f32[16,32,128]{2,1,0:T(8,128)S(1)}, f32[16,32,128]{2,1,0:T(8,128)}, u32[]{:S(2)}) copy-start(f32[16,32,128]{2,1,0:T(8,128)} %b.9) | copy-start | bytes 786436
  1.8 13.8 %collective-permute-start.3 = (f32[13,32,128]{2,1,0:T(8,128)S(1)}, f32[13,32,128]{2,1,0:T(8,128)S(1)}, u32[]{:S(2)}, u32[]{:S(2)}) collective-permute-start(f32[13,32,128]{2,1,0:T(8,128)S(1)} %get-tuple-element.132), channel_id=1, source_target_pairs={{0,8},{1,9},{2,10},{3,11},{4,12},{5,13},{6,14},{7,15},{8,0},{9,1},... | collective-permute-start | bytes 638984 | tf_op jit(solution)/shard_map/ppermute | solution.py:235
  3.8 11.8 %collective-permute-start.2 = (f32[13,32,128]{2,1,0:T(8,128)S(1)}, f32[13,32,128]{2,1,0:T(8,128)S(1)}, u32[]{:S(2)}, u32[]{:S(2)}) collective-permute-start(f32[13,32,128]{2,1,0:T(8,128)S(1)} %get-tuple-element.133), channel_id=1, source_target_pairs={{0,1},{1,0},{2,3},{3,2},{4,5},{5,4},{6,7},{7,6},{8,16},{9,17},{10,... | collective-permute-start | bytes 638984 | tf_op jit(solution)/shard_map/ppermute | solution.py:235
  9.0 5.8 %collective-permute-start = (f32[400,128]{1,0:T(8,128)S(1)}, f32[400,128]{1,0:T(8,128)S(1)}, u32[]{:S(2)}, u32[]{:S(2)}) collective-permute-start(f32[400,128]{1,0:T(8,128)S(1)} %get-tuple-element.67), channel_id=1, source_target_pairs={{0,8},{1,2},{2,1},{3,4},{4,3},{5,6},{6,5},{7,15},{8,0},{9,10},{10,... | collective-permute-start | bytes 614408 | tf_op jit(solution)/shard_map/ppermute | solution.py:235
  9.1 5.7 %collective-permute-start.1 = (f32[400,128]{1,0:T(8,128)S(1)}, f32[400,128]{1,0:T(8,128)S(1)}, u32[]{:S(2)}, u32[]{:S(2)}) collective-permute-start(f32[400,128]{1,0:T(8,128)S(1)} %get-tuple-element.68), channel_id=1, source_target_pairs={{0,1},{1,0},{2,3},{3,2},{4,5},{5,4},{6,7},{7,6},{8,9},{9,8},{10,11... | collective-permute-start | bytes 614408 | tf_op jit(solution)/shard_map/ppermute | solution.py:235
  16.6 5.0 %collective-permute-start.4 = (f32[240,128]{1,0:T(8,128)S(1)}, f32[240,128]{1,0:T(8,128)S(1)}, u32[]{:S(2)}, u32[]{:S(2)}) collective-permute-start(f32[240,128]{1,0:T(8,128)S(1)} %get-tuple-element.88), channel_id=1, source_target_pairs={{0,8},{1,2},{2,1},{3,4},{4,3},{5,6},{6,5},{7,15},{8,0},{9,10},{10,... | collective-permute-start | bytes 368648 | tf_op jit(solution)/shard_map/ppermute | solution.py:235
  16.6 4.9 %collective-permute-start.5 = (f32[240,128]{1,0:T(8,128)S(1)}, f32[240,128]{1,0:T(8,128)S(1)}, u32[]{:S(2)}, u32[]{:S(2)}) collective-permute-start(f32[240,128]{1,0:T(8,128)S(1)} %get-tuple-element.89), channel_id=1, source_target_pairs={{0,1},{1,0},{2,3},{3,2},{4,5},{5,4},{6,7},{7,6},{8,9},{9,8},{10,11... | collective-permute-start | bytes 368648 | tf_op jit(solution)/shard_map/ppermute | solution.py:235
  22.4 6.1 %collective-permute-start.6 = (f32[344,128]{1,0:T(8,128)S(1)}, f32[344,128]{1,0:T(8,128)S(1)}, u32[]{:S(2)}, u32[]{:S(2)}) collective-permute-start(f32[344,128]{1,0:T(8,128)S(1)} %get-tuple-element.107), channel_id=1, source_target_pairs={{0,8},{1,9},{2,10},{3,11},{4,12},{5,13},{6,14},{7,15},{8,0},{9,1},... | collective-permute-start | bytes 528392 | tf_op jit(solution)/shard_map/ppermute | solution.py:235
  22.5 8.6 %collective-permute-start.7 = (f32[344,128]{1,0:T(8,128)S(1)}, f32[344,128]{1,0:T(8,128)S(1)}, u32[]{:S(2)}, u32[]{:S(2)}) collective-permute-start(f32[344,128]{1,0:T(8,128)S(1)} %get-tuple-element.108), channel_id=1, source_target_pairs={{0,1},{1,0},{2,3},{3,2},{4,5},{5,4},{6,7},{7,6},{8,16},{9,17},{10,... | collective-permute-start | bytes 528392 | tf_op jit(solution)/shard_map/ppermute | solution.py:235
  25.8 6.9 %collective-permute-start.8 = (f32[64,128]{1,0:T(8,128)S(1)}, f32[64,128]{1,0:T(8,128)S(1)}, u32[]{:S(2)}, u32[]{:S(2)}) collective-permute-start(f32[64,128]{1,0:T(8,128)S(1)} %get-tuple-element.109), channel_id=1, source_target_pairs={{0,1},{1,0},{2,3},{3,2},{4,5},{5,4},{6,7},{7,6},{8,9},{9,8},{10,11... | collective-permute-start | bytes 98312 | tf_op jit(solution)/shard_map/ppermute | solution.py:235
  27.2 5.5 %collective-permute-start.9 = (f32[64,128]{1,0:T(8,128)S(1)}, f32[64,128]{1,0:T(8,128)S(1)}, u32[]{:S(2)}, u32[]{:S(2)}) collective-permute-start(f32[64,128]{1,0:T(8,128)S(1)} %get-tuple-element.110), channel_id=1, source_target_pairs={{0,16},{1,17},{2,18},{3,19},{4,20},{5,21},{6,22},{7,23},{8,24},{9,... | collective-permute-start | bytes 98312 | tf_op jit(solution)/shard_map/ppermute | solution.py:235

commit v2 on v1

--- a/solution.py
+++ b/solution.py
@@ -97,7 +97,6 @@
         wy[i, at, :] = w_up
         wym[i, at, :] = w_down
         wz[i, at, :] = jnp.where(last, 0.0, w_right)
-        wzm[i, at, :] = jnp.where(first, 0.0, w_left)
         diag[i, at, :] = d
         inv[i, at, :] = iv
         if rhs is not None:
@@ -124,7 +123,7 @@
         nxt, wx_next = src[i + 1, dom, :], wx[i, at, :]
         t = wx_next * nxt + wx_prev * prev
         t = t + wy[i, at, :] * src[i, pl.ds(9 + lo, n), :] + wym[i, at, :] * src[i, pl.ds(7 + lo, n), :]
-        t = t + wz[i, at, :] * roll(cur, -rep) + wzm[i, at, :] * roll(cur, rep)
+        t = t + wz[i, at, :] * roll(cur, -rep) + roll(wz[i, at, :] * cur, rep)
         emit(i, lo, n, cur, rhs_n[i, at, :] + inv[i, at, :] * t - cur)
         prev, cur, wx_prev = cur, nxt, wx_next
 

time: 34.3 us -> 34.3 us (level)
  no operation moved by 1% of the time
where the time goes in v2:
time: 34.3 us; the launch traced here: 34.2 us
  starting transfers between devices  15.1 us (44%)
  waiting for transfers between devices  11 us (32%)
  Pallas kernels  6.23 us (18%)
  local copies, waits for them, and re-layouts  1.07 us (3%)
  between operations  0.78 us (2%)
    ppermute x5, waiting for transfers between devices, swaps(): lax.ppermute(first, axes, orders[0])  8.39 us
    ppermute x5, starting transfers between devices, swaps(): lax.ppermute(second, axes, orders[1])  8.21 us
    ppermute x5, starting transfers between devices, swaps(): lax.ppermute(first, axes, orders[0])  6.85 us
    pallas_call x7, Pallas kernels, call(): pl.pallas_call(kernel, out_shape=[jax.ShapeDtypeStruct(s, F32) for s in o...  6.23 us
    ppermute x5, waiting for transfers between devices, swaps(): lax.ppermute(second, axes, orders[1])  2.61 us
    slice x3, local copies, waits for them, and re-layouts, pack_fine_x(): f[16 - n:]  0.96 us
  transfers between devices with their start and end apart: 10, of which 5 were waited for; matrix products, arithmetic and copies ran while one was open for 0% of the time, Pallas kernels for 9%

profile of v2, /device:TPU:24, one launch (start us, length us, event | category | flops | bytes accessed | tf_op | source)
XLA Modules:
  0.0 34.2 jit_solution(2145591398489307960)
XLA Ops:
  0.7 0.9 %fusion = (f32[4,32,128]{2,1,0:T(8,128)S(1)}, f32[4,32,128]{2,1,0:T(8,128)S(1)}) fusion(f32[16,32,128]{2,1,0:T(8,128)} %b.9), kind=kLoop, calls=%fused_computation.4 | loop fusion | bytes 262144 | tf_op jit(solution)/shard_map/slice | solution.py:242
  1.6 0.1 copy-done
  1.8 0.0 copy-start.1
  1.8 2.0 %collective-permute-start.3 = (f32[13,32,128]{2,1,0:T(8,128)S(1)}, f32[13,32,128]{2,1,0:T(8,128)S(1)}, u32[]{:S(2)}, u32[]{:S(2)}) collective-permute-start(f32[13,32,128]{2,1,0:T(8,128)S(1)} %get-tuple-element.132), channel_id=1, source_target_pairs={{0,8},{1,9},{2,10},{3,11},{4,12},{5,13},{6,14},{7,15},{8,0},{9,1},... | collective-permute-start | bytes 638984 | tf_op jit(solution)/shard_map/ppermute | solution.py:234
  3.8 5.1 %collective-permute-start.2 = (f32[13,32,128]{2,1,0:T(8,128)S(1)}, f32[13,32,128]{2,1,0:T(8,128)S(1)}, u32[]{:S(2)}, u32[]{:S(2)}) collective-permute-start(f32[13,32,128]{2,1,0:T(8,128)S(1)} %get-tuple-element.133), channel_id=1, source_target_pairs={{0,1},{1,0},{2,3},{3,2},{4,5},{5,4},{6,7},{7,6},{8,16},{9,17},{10,... | collective-permute-start | bytes 638984 | tf_op jit(solution)/shard_map/ppermute | solution.py:234
  9.0 0.1 collective-permute-start
  9.1 1.6 %collective-permute-start.1 = (f32[400,128]{1,0:T(8,128)S(1)}, f32[400,128]{1,0:T(8,128)S(1)}, u32[]{:S(2)}, u32[]{:S(2)}) collective-permute-start(f32[400,128]{1,0:T(8,128)S(1)} %get-tuple-element.68), channel_id=1, source_target_pairs={{0,1},{1,0},{2,3},{3,2},{4,5},{5,4},{6,7},{7,6},{8,9},{9,8},{10,11... | collective-permute-start | bytes 614408 | tf_op jit(solution)/shard_map/ppermute | solution.py:234
  10.7 4.2 %collective-permute-done.ya_in = f32[400,128]{1,0:T(8,128)S(1)} collective-permute-done((f32[400,128]{1,0:T(8,128)S(1)}, f32[400,128]{1,0:T(8,128)S(1)}, u32[]{:S(2)}, u32[]{:S(2)}) %collective-permute-start) | collective-permute-done | bytes 204832 | tf_op jit(solution)/shard_map/ppermute | solution.py:234
  14.9 0.8 %shard_map.51 = (f32[24,32,128]{2,1,0:T(8,128)S(1)}, f32[24,32,128]{2,1,0:T(8,128)S(1)}, f32[24,32,128]{2,1,0:T(8,128)S(1)}, f32[24,32,128]{2,1,0:T(8,128)S(1)},...) custom-call(f32[16,32,128]{2,1,0:T(8,128)S(1)} %copy-done.1, ...), custom_call_target="tpu_custom_call" | custom-call | tf_op jit(solution)/shard_map/pallas_call | solution.py:622
  15.6 0.9 %shard_map.52 = (f32[16,32,128]{2,1,0:T(8,128)S(1)}, f32[8,8,128]{2,1,0:T(8,128)S(1)}, f32[240,128]{1,0:T(8,128)S(1)}, f32[240,128]{1,0:T(8,128)S(1)}) custom-call(f32[16,32,128]{2,1,0:T(8,128)S(1)} %copy-done.1, f32[16,32,128]{2,1,0:T(8,128)S(1)} %copy-done, f32[16,32,128]{2,1,0:T(8,128)S(1)} %copy-done.2, ...), custom_call_target="tpu_custom_call" | custom-call | tf_op jit(solution)/shard_map/pallas_call | solution.py:622
  16.6 0.1 collective-permute-start.4
  16.6 1.0 %collective-permute-start.5 = (f32[240,128]{1,0:T(8,128)S(1)}, f32[240,128]{1,0:T(8,128)S(1)}, u32[]{:S(2)}, u32[]{:S(2)}) collective-permute-start(f32[240,128]{1,0:T(8,128)S(1)} %get-tuple-element.89), channel_id=1, source_target_pairs={{0,1},{1,0},{2,3},{3,2},{4,5},{5,4},{6,7},{7,6},{8,9},{9,8},{10,11... | collective-permute-start | bytes 368648 | tf_op jit(solution)/shard_map/ppermute | solution.py:234
  17.7 0.8 %shard_map.53 = (f32[24,40,128]{2,1,0:T(8,128)S(1)}, f32[24,40,128]{2,1,0:T(8,128)S(1)}, f32[24,40,128]{2,1,0:T(8,128)S(1)}, f32[24,40,128]{2,1,0:T(8,128)S(1)},...) custom-call(f32[16,32,128]{2,1,0:T(8,128)S(1)} %copy-done.1, ...), custom_call_target="tpu_custom_call" | custom-call | tf_op jit(solution)/shard_map/pallas_call | solution.py:622
  18.5 3.0 %collective-permute-done.4.ya2 = f32[240,128]{1,0:T(8,128)S(1)} collective-permute-done((f32[240,128]{1,0:T(8,128)S(1)}, f32[240,128]{1,0:T(8,128)S(1)}, u32[]{:S(2)}, u32[]{:S(2)}) %collective-permute-start.4) | collective-permute-done | bytes 122912 | tf_op jit(solution)/shard_map/ppermute | solution.py:234
  21.5 0.9 %shard_map.54 = (f32[16,8,128]{2,1,0:T(8,128)S(1)}, f32[3,8,24,128]{3,2,1,0:T(8,128)S(1)}, f32[344,128]{1,0:T(8,128)S(1)}, f32[344,128]{1,0:T(8,128)S(1)}, f32[64,128]{1,0:T(8,128)S(1)}, /*index=5*/f32[64,128]{1,0:T(8,128)S(1)}) custom-call(f32[16,32,128]{2,1,0:T(8,128)S(1)} %copy-done.1, f32[16,32,128]{2,1,0:T(8,128)S(1)} %copy-done, ...), custom_call_target="tpu_custom_call" | custom-call | tf_op jit(solution)/shard_map/pallas_call | solution.py:622
  22.4 0.1 collective-permute-start.6
  22.5 3.3 %collective-permute-start.7 = (f32[344,128]{1,0:T(8,128)S(1)}, f32[344,128]{1,0:T(8,128)S(1)}, u32[]{:S(2)}, u32[]{:S(2)}) collective-permute-start(f32[344,128]{1,0:T(8,128)S(1)} %get-tuple-element.108), channel_id=1, source_target_pairs={{0,1},{1,0},{2,3},{3,2},{4,5},{5,4},{6,7},{7,6},{8,16},{9,17},{10,... | collective-permute-start | bytes 528392 | tf_op jit(solution)/shard_map/ppermute | solution.py:234
  25.8 1.5 %collective-permute-start.8 = (f32[64,128]{1,0:T(8,128)S(1)}, f32[64,128]{1,0:T(8,128)S(1)}, u32[]{:S(2)}, u32[]{:S(2)}) collective-permute-start(f32[64,128]{1,0:T(8,128)S(1)} %get-tuple-element.109), channel_id=1, source_target_pairs={{0,1},{1,0},{2,3},{3,2},{4,5},{5,4},{6,7},{7,6},{8,9},{9,8},{10,11... | collective-permute-start | bytes 98312 | tf_op jit(solution)/shard_map/ppermute | solution.py:234
  27.2 0.3 collective-permute-start.9
  27.6 0.9 %collective-permute-done.6.near_a = f32[344,128]{1,0:T(8,128)S(1)} collective-permute-done((f32[344,128]{1,0:T(8,128)S(1)}, f32[344,128]{1,0:T(8,128)S(1)}, u32[]{:S(2)}, u32[]{:S(2)}) %collective-permute-start.6) | collective-permute-done | bytes 176160 | tf_op jit(solution)/shard_map/ppermute | solution.py:234
  28.5 2.6 %collective-permute-done.7.near_b = f32[344,128]{1,0:T(8,128)S(1)} collective-permute-done((f32[344,128]{1,0:T(8,128)S(1)}, f32[344,128]{1,0:T(8,128)S(1)}, u32[]{:S(2)}, u32[]{:S(2)}) %collective-permute-start.7) | collective-permute-done | bytes 176160 | tf_op jit(solution)/shard_map/ppermute | solution.py:234
  31.1 1.3 %shard_map.55 = (f32[14,40,128]{2,1,0:T(8,128)S(1)}, f32[14,40,128]{2,1,0:T(8,128)S(1)}, f32[14,40,128]{2,1,0:T(8,128)S(1)}, f32[14,40,128]{2,1,0:T(8,128)S(1)},...) custom-call(f32[3,8,24,128]{3,2,1,0:T(8,128)S(1)} %get-tuple-element, ...), custom_call_target="tpu_custom_call" | custom-call | tf_op jit(solution)/shard_map/pallas_call | solution.py:622
  32.4 0.3 collective-permute-done.8.far_a
  32.7 1.5 %shard_map.56 = (f32[16,32,128]{2,1,0:T(8,128)}, f32[8,16,64]{2,1,0:T(8,128)}) custom-call(f32[16,32,128]{2,1,0:T(8,128)S(1)} %get-tuple-element.86.x_fine, f32[16,8,128]{2,1,0:T(8,128)S(1)} %get-tuple-element.105.x_edge, f32[3,8,24,128]{3,2,1,0:T(8,128)S(1)} %get-tuple-element.106.ext, f32[344,128]{1,0:T(8,128)S(1)} %collective-permute-done.6.near_a, ...), custom_call_target="tpu_custom_call" | custom-call | tf_op jit(solution)/shard_map/pallas_call | solution.py:622
  (14 shorter events, 0.2 us)
Async XLA Ops:
  0.6 1.0 %copy-start.2 = (f32[16,32,128]{2,1,0:T(8,128)S(1)}, f32[16,32,128]{2,1,0:T(8,128)}, u32[]{:S(2)}) copy-start(f32[16,32,128]{2,1,0:T(8,128)} %shift.9) | copy-start | bytes 786436
  0.6 1.1 %copy-start = (f32[16,32,128]{2,1,0:T(8,128)S(1)}, f32[16,32,128]{2,1,0:T(8,128)}, u32[]{:S(2)}) copy-start(f32[16,32,128]{2,1,0:T(8,128)} %beta.9) | copy-start | bytes 786436
  1.8 7.2 %copy-start.1 = (f32[16,32,128]{2,1,0:T(8,128)S(1)}, f32[16,32,128]{2,1,0:T(8,128)}, u32[]{:S(2)}) copy-start(f32[16,32,128]{2,1,0:T(8,128)} %b.9) | copy-start | bytes 786436
  1.8 13.8 %collective-permute-start.3 = (f32[13,32,128]{2,1,0:T(8,128)S(1)}, f32[13,32,128]{2,1,0:T(8,128)S(1)}, u32[]{:S(2)}, u32[]{:S(2)}) collective-permute-start(f32[13,32,128]{2,1,0:T(8,128)S(1)} %get-tuple-element.132), channel_id=1, source_target_pairs={{0,8},{1,9},{2,10},{3,11},{4,12},{5,13},{6,14},{7,15},{8,0},{9,1},... | collective-permute-start | bytes 638984 | tf_op jit(solution)/shard_map/ppermute | solution.py:234
  3.8 11.8 %collective-permute-start.2 = (f32[13,32,128]{2,1,0:T(8,128)S(1)}, f32[13,32,128]{2,1,0:T(8,128)S(1)}, u32[]{:S(2)}, u32[]{:S(2)}) collective-permute-start(f32[13,32,128]{2,1,0:T(8,128)S(1)} %get-tuple-element.133), channel_id=1, source_target_pairs={{0,1},{1,0},{2,3},{3,2},{4,5},{5,4},{6,7},{7,6},{8,16},{9,17},{10,... | collective-permute-start | bytes 638984 | tf_op jit(solution)/shard_map/ppermute | solution.py:234
  9.0 5.8 %collective-permute-start = (f32[400,128]{1,0:T(8,128)S(1)}, f32[400,128]{1,0:T(8,128)S(1)}, u32[]{:S(2)}, u32[]{:S(2)}) collective-permute-start(f32[400,128]{1,0:T(8,128)S(1)} %get-tuple-element.67), channel_id=1, source_target_pairs={{0,8},{1,2},{2,1},{3,4},{4,3},{5,6},{6,5},{7,15},{8,0},{9,10},{10,... | collective-permute-start | bytes 614408 | tf_op jit(solution)/shard_map/ppermute | solution.py:234
  9.1 5.7 %collective-permute-start.1 = (f32[400,128]{1,0:T(8,128)S(1)}, f32[400,128]{1,0:T(8,128)S(1)}, u32[]{:S(2)}, u32[]{:S(2)}) collective-permute-start(f32[400,128]{1,0:T(8,128)S(1)} %get-tuple-element.68), channel_id=1, source_target_pairs={{0,1},{1,0},{2,3},{3,2},{4,5},{5,4},{6,7},{7,6},{8,9},{9,8},{10,11... | collective-permute-start | bytes 614408 | tf_op jit(solution)/shard_map/ppermute | solution.py:234
  16.6 5.0 %collective-permute-start.4 = (f32[240,128]{1,0:T(8,128)S(1)}, f32[240,128]{1,0:T(8,128)S(1)}, u32[]{:S(2)}, u32[]{:S(2)}) collective-permute-start(f32[240,128]{1,0:T(8,128)S(1)} %get-tuple-element.88), channel_id=1, source_target_pairs={{0,8},{1,2},{2,1},{3,4},{4,3},{5,6},{6,5},{7,15},{8,0},{9,10},{10,... | collective-permute-start | bytes 368648 | tf_op jit(solution)/shard_map/ppermute | solution.py:234
  16.6 4.9 %collective-permute-start.5 = (f32[240,128]{1,0:T(8,128)S(1)}, f32[240,128]{1,0:T(8,128)S(1)}, u32[]{:S(2)}, u32[]{:S(2)}) collective-permute-start(f32[240,128]{1,0:T(8,128)S(1)} %get-tuple-element.89), channel_id=1, source_target_pairs={{0,1},{1,0},{2,3},{3,2},{4,5},{5,4},{6,7},{7,6},{8,9},{9,8},{10,11... | collective-permute-start | bytes 368648 | tf_op jit(solution)/shard_map/ppermute | solution.py:234
  22.4 6.1 %collective-permute-start.6 = (f32[344,128]{1,0:T(8,128)S(1)}, f32[344,128]{1,0:T(8,128)S(1)}, u32[]{:S(2)}, u32[]{:S(2)}) collective-permute-start(f32[344,128]{1,0:T(8,128)S(1)} %get-tuple-element.107), channel_id=1, source_target_pairs={{0,8},{1,9},{2,10},{3,11},{4,12},{5,13},{6,14},{7,15},{8,0},{9,1},... | collective-permute-start | bytes 528392 | tf_op jit(solution)/shard_map/ppermute | solution.py:234
  22.5 8.6 %collective-permute-start.7 = (f32[344,128]{1,0:T(8,128)S(1)}, f32[344,128]{1,0:T(8,128)S(1)}, u32[]{:S(2)}, u32[]{:S(2)}) collective-permute-start(f32[344,128]{1,0:T(8,128)S(1)} %get-tuple-element.108), channel_id=1, source_target_pairs={{0,1},{1,0},{2,3},{3,2},{4,5},{5,4},{6,7},{7,6},{8,16},{9,17},{10,... | collective-permute-start | bytes 528392 | tf_op jit(solution)/shard_map/ppermute | solution.py:234
  25.8 6.9 %collective-permute-start.8 = (f32[64,128]{1,0:T(8,128)S(1)}, f32[64,128]{1,0:T(8,128)S(1)}, u32[]{:S(2)}, u32[]{:S(2)}) collective-permute-start(f32[64,128]{1,0:T(8,128)S(1)} %get-tuple-element.109), channel_id=1, source_target_pairs={{0,1},{1,0},{2,3},{3,2},{4,5},{5,4},{6,7},{7,6},{8,9},{9,8},{10,11... | collective-permute-start | bytes 98312 | tf_op jit(solution)/shard_map/ppermute | solution.py:234
  27.2 5.5 %collective-permute-start.9 = (f32[64,128]{1,0:T(8,128)S(1)}, f32[64,128]{1,0:T(8,128)S(1)}, u32[]{:S(2)}, u32[]{:S(2)}) collective-permute-start(f32[64,128]{1,0:T(8,128)S(1)} %get-tuple-element.110), channel_id=1, source_target_pairs={{0,16},{1,17},{2,18},{3,19},{4,20},{5,21},{6,22},{7,23},{8,24},{9,... | collective-permute-start | bytes 98312 | tf_op jit(solution)/shard_map/ppermute | solution.py:234
